TPU v7x, 256 devices: a whole 4x4x8 slice. The times are simulated.
256 devices in a mesh: row: 8 (over y, core), col: 16 (over z, x_hi), depth: 2 (over x_lo).
Axes of the slice: x: 4 (x_hi: 2, x_lo: 2; x = x_hi * 2 + x_lo), y: 4, z: 8, core: 2. Of those that a mesh axis runs over, the one named last changes fastest.
Arguments:
- a_blocks: float32 [192, 16, 128, 128], P('row', 'col'), may hold values from -6 to 6
- a_index: int32 [2, 192, 16], P(None, 'row', 'col'), may hold values from -1 to 383, as said below
- b_blocks: float32 [2, 64, 16, 128, 128], P(None, 'row', 'col'), may hold values from -0.5 to 0.5
- b_index: int32 [2, 2, 64, 16], P(None, None, 'row', 'col'), may hold values from -1 to 383, as said below
- c_index: int32 [2, 256, 16], P(None, 'row', 'col'), may hold values from -1 to 383, as said below
Outputs:
- c_blocks: float32 [256, 16, 128, 128], P('row', 'col')
Inputs may be any that keep to these rules, and one draw needn't show every extreme that they name: `a_index`: A slot's two entries are both -1 (empty) or both live; a live slot of slot group r and column g names a block row of row group r (rows r * 48 to (r + 1) * 48 - 1) and an inner index of inner group g (g * 24 to (g + 1) * 24 - 1); no block is named twice; every group pair holds 12 to 24 live slots, and some pair holds 24. `b_index`: slots are both -1 or both live; a live slot of half h, slot group r, column c names an inner index of inner group h * 8 + r and a block column of column group c (c * 24 to (c + 1) * 24 - 1); no block is named twice; in every group pair at most 2 live blocks share one inner index, and in each pair some inner index is shared by exactly 2 live blocks. `c_index`: slots are both -1 or both live; a live slot of slot group r and column c names a block row of row group r and a block column of column group c; no block is named twice; every group pair holds 16 to 32 live slots, and some pair holds 32.
All inputs are finite; a program needn't handle non-finite values.
Results may differ from a plain program's by a relative error of at most 0.0003.
Values sent between devices are 32-bit elements; how exact they have to be, the bound alone decides.
A program may use at most 128 MiB of HBM per device.

v0:
```python
import jax
import jax.numpy as jnp
from jax import lax
from jax.sharding import PartitionSpec as P

MATCH = 2


PRECISE = lax.Precision.HIGHEST


def from_behind(value, axis, by):
    size = lax.axis_size(axis)
    return lax.ppermute(value, axis, [(i, (i + by) % size) for i in range(size)])


def tile_product(
    partial_value, row_tiles, row_ids, inner_ids, col_tiles, inner_keys, col_ids, out_rows, out_cols
):
    pairing = (inner_ids[:, None] == inner_keys[None, :]) & (inner_ids[:, None] >= 0)
    ranking = jnp.cumsum(pairing.astype(jnp.int32), axis=1) - 1
    positions = jnp.arange(MATCH, dtype=jnp.int32)
    chooser = pairing[:, None, :] & (ranking[:, None, :] == positions[None, :, None])
    one_hot = chooser.astype(jnp.float32)
    gathered = jnp.einsum("amb,bxy->amxy", one_hot, col_tiles, precision=PRECISE)
    target = jnp.sum(jnp.where(chooser, col_ids[None, None, :], 0), axis=2).astype(jnp.int32)
    usable = jnp.any(chooser, axis=2)
    products = jnp.einsum("axy,amyz->amxz", row_tiles, gathered, precision=PRECISE)
    routing = (out_rows[:, None, None] == row_ids[None, :, None]) & (
        out_cols[:, None, None] == target[None, :, :]
    )
    routing = routing & usable[None, :, :] & (out_rows[:, None, None] >= 0)
    return partial_value + jnp.einsum(
        "cam,amxz->cxz", routing.astype(jnp.float32), products, precision=PRECISE
    )


def keep_where(chosen, incoming, current):
    return tuple(
        (
            jnp.where(chosen, fresh_part, held_part)
            for fresh_part, held_part in zip(incoming, current)
        )
    )


def local(a_blocks, a_index, b_blocks, b_index, c_index):
    row_tiles = a_blocks[:, 0]
    row_ids = a_index[0, :, 0]
    inner_ids = a_index[1, :, 0]
    tile_width = b_blocks.shape[-1]
    out_rows = c_index[0, :, 0]
    out_cols = c_index[1, :, 0]
    rows_count = lax.axis_size("row")
    cols_count = lax.axis_size("col")
    depth_count = lax.axis_size("depth")
    steps_count = cols_count // depth_count
    layer_index = lax.axis_index("depth")
    partial_value = jnp.zeros((out_rows.shape[0], tile_width, tile_width), jnp.float32)
    col_tiles = b_blocks[:, :, 0].reshape(-1, tile_width, tile_width)
    inner_keys = b_index[0, :, :, 0].reshape(-1)
    col_ids = b_index[1, :, :, 0].reshape(-1)
    row_lift = (lax.axis_index("row") + layer_index * steps_count) % cols_count
    for power in range((cols_count - 1).bit_length()):
        arrived = from_behind((row_tiles, row_ids, inner_ids), "col", -(1 << power))
        chosen = row_lift >> power & 1 == 1
        row_tiles, row_ids, inner_ids = keep_where(chosen, arrived, (row_tiles, row_ids, inner_ids))
    col_lift = (lax.axis_index("col") + layer_index * steps_count) % rows_count
    for power in range((rows_count - 1).bit_length()):
        arrived = from_behind((col_tiles, inner_keys, col_ids), "row", -(1 << power))
        chosen = col_lift >> power & 1 == 1
        col_tiles, inner_keys, col_ids = keep_where(
            chosen, arrived, (col_tiles, inner_keys, col_ids)
        )
    for section in range(steps_count):
        partial_value = tile_product(
            partial_value,
            row_tiles,
            row_ids,
            inner_ids,
            col_tiles,
            inner_keys,
            col_ids,
            out_rows,
            out_cols,
        )
        if section + 1 < steps_count:
            row_tiles, row_ids, inner_ids = from_behind((row_tiles, row_ids, inner_ids), "col", -1)
            col_tiles, inner_keys, col_ids = from_behind(
                (col_tiles, inner_keys, col_ids), "row", -1
            )
    summed = lax.psum(partial_value, "depth")
    return summed[:, None]


def solution(mesh):
    in_specs = (
        P("row", "col", None, None),
        P(None, "row", "col"),
        P(None, "row", "col", None, None),
        P(None, None, "row", "col"),
        P(None, "row", "col"),
    )
    out_specs = P("row", "col", None, None)
    return jax.shard_map(local, mesh=mesh, in_specs=in_specs, out_specs=out_specs, check_vma=False)
```

profile of v0, /device:TPU:1, one launch (start us, length us, event | category | flops | bytes accessed | tf_op | source)
XLA Modules:
  0.0 676.3 jit_solution(8634117304896854595)
XLA Ops:
  6.5 8.9 %collective-permute-start.17 = (f32[24,128,128]{2,1,0:T(8,128)}, f32[24,128,128]{2,1,0:T(8,128)S(1)}, u32[]{:S(2)}, u32[]{:S(2)}) collective-permute-start(f32[24,128,128]{2,1,0:T(8,128)} %bitcast.197), channel_id=1, source_target_pairs={{0,30},{2,0},{4,2},{6,4},{8,6},{10,8},{12,10},{14,12},{16,14},{18,... | collective-permute-start | bytes 4718600 | tf_op jit(solution)/shard_map/ppermute | solution.py:14
  38.6 10.2 %collective-permute-done = s32[24]{0:T(128)S(1)} collective-permute-done((s32[24]{0:T(128)S(1)}, s32[24]{0:T(128)S(1)}, u32[]{:S(2)}, u32[]{:S(2)}) %collective-permute-start) | collective-permute-done | bytes 128 | tf_op jit(solution)/shard_map/ppermute | solution.py:14
  68.9 28.3 %collective-permute-done.6 = s32[24]{0:T(128)S(1)} collective-permute-done((s32[24]{0:T(128)S(1)}, s32[24]{0:T(128)S(1)}, u32[]{:S(2)}, u32[]{:S(2)}) %collective-permute-start.6) | collective-permute-done | bytes 128 | tf_op jit(solution)/shard_map/ppermute | solution.py:14
  110.3 5.8 collective-permute-start.22
  125.0 33.9 %collective-permute-done.21 = s32[24]{0:T(128)S(1)} collective-permute-done((s32[24]{0:T(128)S(1)}, s32[24]{0:T(128)S(1)}, u32[]{:S(2)}, u32[]{:S(2)}) %collective-permute-start.21) | collective-permute-done | bytes 128 | tf_op jit(solution)/shard_map/ppermute | solution.py:14
  158.9 5.5 collective-permute-start.28
  164.4 24.3 %collective-permute-start.27 = (s32[24]{0:T(128)S(1)}, s32[24]{0:T(128)S(1)}, u32[]{:S(2)}, u32[]{:S(2)}) collective-permute-start(s32[24]{0:T(128)S(1)} %collective-permute-done.21), channel_id=1, source_target_pairs={{0,30},{2,0},{4,2},{6,4},{8,6},{10,8},{12,10},{14,12},{16,14},{18,... | collective-permute-start | bytes 296 | tf_op jit(solution)/shard_map/ppermute | solution.py:14
  209.7 7.9 %collective-permute-done.15 = f32[16,128,128]{2,1,0:T(8,128)} collective-permute-done((f32[16,128,128]{2,1,0:T(8,128)}, f32[16,128,128]{2,1,0:T(8,128)}, u32[]{:S(2)}, u32[]{:S(2)}) %collective-permute-start.15) | collective-permute-done | bytes 1048608 | tf_op jit(solution)/shard_map/ppermute | solution.py:14
  221.0 45.5 %collective-permute-done.20 = f32[24,128,128]{2,1,0:T(8,128)} collective-permute-done((f32[24,128,128]{2,1,0:T(8,128)S(1)}, f32[24,128,128]{2,1,0:T(8,128)}, u32[]{:S(2)}, u32[]{:S(2)}) %collective-permute-start.20) | collective-permute-done | bytes 1572896 | tf_op jit(solution)/shard_map/ppermute | solution.py:14
  271.2 38.7 %collective-permute-done.40 = s32[24]{0:T(128)S(1)} collective-permute-done((s32[24]{0:T(128)S(1)}, s32[24]{0:T(128)S(1)}, u32[]{:S(2)}, u32[]{:S(2)}) %collective-permute-start.40) | collective-permute-done | bytes 128 | tf_op jit(solution)/shard_map/ppermute | solution.py:14
  329.9 26.5 %collective-permute-done.52 = s32[24]{0:T(128)S(1)} collective-permute-done((s32[24]{0:T(128)S(1)}, s32[24]{0:T(128)S(1)}, u32[]{:S(2)}, u32[]{:S(2)}) %collective-permute-start.52) | collective-permute-done | bytes 128 | tf_op jit(solution)/shard_map/ppermute | solution.py:14
  369.9 25.4 %collective-permute-done.58 = s32[24]{0:T(128)S(1)} collective-permute-done((s32[24]{0:T(128)S(1)}, s32[24]{0:T(128)S(1)}, u32[]{:S(2)}, u32[]{:S(2)}) %collective-permute-start.58) | collective-permute-done | bytes 128 | tf_op jit(solution)/shard_map/ppermute | solution.py:14
  406.8 5.8 collective-permute-start.44
  422.3 7.3 %fusion.30 = f32[24,2,128,128]{3,2,1,0:T(8,128)} fusion(f32[24,2,128,128]{3,0,2,1:T(8,128)S(1)} %fusion.57, f32[24,128,128]{2,1,0:T(8,128)S(1)} %broadcast_select_fusion.3), kind=kOutput, calls=%fused_computation.30 | convolution fusion | flops 1207959552 | bytes 7864320 | tf_op jit(solution)/shard_map/axy,amyz->amxz/dot_general | solution.py:28
  446.8 5.8 collective-permute-start.50
  452.6 8.2 %fusion.28 = f32[24,2,128,128]{3,2,1,0:T(8,128)} fusion(f32[24,2,128,128]{3,0,2,1:T(8,128)S(1)} %copy-done.6, f32[24,128,128]{2,1,0:T(8,128)} %collective-permute-done.26), kind=kOutput, calls=%fused_computation.28 | convolution fusion | flops 1207959552 | bytes 7864320 | tf_op jit(solution)/shard_map/axy,amyz->amxz/dot_general | solution.py:28
  479.4 8.2 %fusion.26 = f32[24,2,128,128]{3,2,1,0:T(8,128)} fusion(f32[24,2,128,128]{3,0,2,1:T(8,128)S(1)} %copy-done.4, f32[24,128,128]{2,1,0:T(8,128)} %collective-permute-done.32), kind=kOutput, calls=%fused_computation.26 | convolution fusion | flops 1207959552 | bytes 7864320 | tf_op jit(solution)/shard_map/axy,amyz->amxz/dot_general | solution.py:28
  501.3 8.2 %fusion.24 = f32[24,2,128,128]{3,2,1,0:T(8,128)} fusion(f32[24,2,128,128]{3,0,2,1:T(8,128)S(1)} %copy-done.1, f32[24,128,128]{2,1,0:T(8,128)} %collective-permute-done.38), kind=kOutput, calls=%fused_computation.24 | convolution fusion | flops 1207959552 | bytes 7864320 | tf_op jit(solution)/shard_map/axy,amyz->amxz/dot_general | solution.py:28
  517.8 8.2 %fusion.22 = f32[24,2,128,128]{3,2,1,0:T(8,128)} fusion(f32[24,2,128,128]{3,0,2,1:T(8,128)S(1)} %copy-done, f32[24,128,128]{2,1,0:T(8,128)} %collective-permute-done.44), kind=kOutput, calls=%fused_computation.22 | convolution fusion | flops 1207959552 | bytes 7864320 | tf_op jit(solution)/shard_map/axy,amyz->amxz/dot_general | solution.py:28
  537.4 8.4 %fusion.20 = f32[24,2,128,128]{3,2,1,0:T(8,128)} fusion(f32[24,2,128,128]{3,0,2,1:T(8,128)S(1)} %copy-done.2, f32[24,128,128]{2,1,0:T(8,128)} %collective-permute-done.50), kind=kOutput, calls=%fused_computation.20 | convolution fusion | flops 1207959552 | bytes 7864320 | tf_op jit(solution)/shard_map/axy,amyz->amxz/dot_general | solution.py:28
  554.2 8.2 %fusion.18 = f32[24,2,128,128]{3,2,1,0:T(8,128)} fusion(f32[24,2,128,128]{3,0,2,1:T(8,128)S(1)} %copy-done.3, f32[24,128,128]{2,1,0:T(8,128)} %collective-permute-done.56), kind=kOutput, calls=%fused_computation.18 | convolution fusion | flops 1207959552 | bytes 7864320 | tf_op jit(solution)/shard_map/axy,amyz->amxz/dot_general | solution.py:28
  570.7 8.2 %fusion.16 = f32[24,2,128,128]{3,2,1,0:T(8,128)} fusion(f32[24,2,128,128]{3,0,2,1:T(8,128)S(1)} %copy-done.5, f32[24,128,128]{2,1,0:T(8,128)} %collective-permute-done.62), kind=kOutput, calls=%fused_computation.16 | convolution fusion | flops 1207959552 | bytes 7864320 | tf_op jit(solution)/shard_map/axy,amyz->amxz/dot_general | solution.py:28
  586.2 7.3 %fusion.32 = f32[32,1,128,128]{3,0,2,1:T(8,128)} fusion(f32[32,128,128,1]{2,0,3,1:T(8,128)S(1)} %fusion, f32[32,128,128,1]{2,0,3,1:T(8,128)} %fusion.2, f32[32,128,128,1]{2,0,3,1:T(8,128)} %fusion.4, f32[32,128,128,1]{2,0,3,1:T(8,128)} %fusion.6, f32[32,128,128,1]{2,0,3,1:T(8,128)} %fusion.8, f32[32,128,128,1]{2,0,3,1:T(8,128)S(1)} %copy-done.8, ...), kind=kOutput, calls=%fused_computation.33 | convolution fusion | flops 305666048 | bytes 19924112 | tf_op jit(solution)/shard_map/cam,amxz->cxz/dot_general | solution.py:33
  593.6 71.4 %all-reduce.2.cloned.1.call-done = f32[32,1,128,128]{3,0,2,1:T(8,128)} async-done(((f32[32,1,128,128]{3,0,2,1:T(8,128)}), f32[32,1,128,128]{3,0,2,1:T(8,128)}) %all-reduce.2.cloned.1.call-update) | async-done | bytes 2097168 | tf_op jit(solution)/shard_map/psum | solution.py:92
  (250 shorter events, 246.1 us)
Async XLA Ops:
  6.5 658.4 %all-reduce.2.cloned.1.call-start = ((), (), s32[]{:S(2)}) async-start(), calls=%async_computation | async-start | bytes 4194304 | tf_op jit(solution)/shard_map/psum | solution.py:92
  6.5 51.8 %collective-permute-start.17 = (f32[24,128,128]{2,1,0:T(8,128)}, f32[24,128,128]{2,1,0:T(8,128)S(1)}, u32[]{:S(2)}, u32[]{:S(2)}) collective-permute-start(f32[24,128,128]{2,1,0:T(8,128)} %bitcast.197), channel_id=1, source_target_pairs={{0,30},{2,0},{4,2},{6,4},{8,6},{10,8},{12,10},{14,12},{16,14},{18,... | collective-permute-start | bytes 4718600 | tf_op jit(solution)/shard_map/ppermute | solution.py:14
  15.4 149.0 %collective-permute-start.14 = (f32[16,128,128]{2,1,0:T(8,128)}, f32[16,128,128]{2,1,0:T(8,128)}, u32[]{:S(2)}, u32[]{:S(2)}) collective-permute-start(f32[16,128,128]{2,1,0:T(8,128)} %bitcast.198), channel_id=1, source_target_pairs={{0,224},{32,0},{64,32},{96,64},{128,96},{160,128},{192,160},{224,1... | collective-permute-start | bytes 3145736 | tf_op jit(solution)/shard_map/ppermute | solution.py:14
  63.8 45.3 %collective-permute-start.18 = (f32[24,128,128]{2,1,0:T(8,128)S(1)}, f32[24,128,128]{2,1,0:T(8,128)S(1)}, u32[]{:S(2)}, u32[]{:S(2)}) collective-permute-start(f32[24,128,128]{2,1,0:T(8,128)S(1)} %broadcast_select_fusion), channel_id=1, source_target_pairs={{0,28},{2,30},{4,0},{6,2},{8,4},{10,6},{12,8},{14,10},{16,12},{18,... | collective-permute-start | bytes 4718600 | tf_op jit(solution)/shard_map/ppermute | solution.py:14
  116.3 74.7 %collective-permute-start.19 = (f32[24,128,128]{2,1,0:T(8,128)S(1)}, f32[24,128,128]{2,1,0:T(8,128)S(1)}, u32[]{:S(2)}, u32[]{:S(2)}) collective-permute-start(f32[24,128,128]{2,1,0:T(8,128)S(1)} %broadcast_select_fusion.1), channel_id=1, source_target_pairs={{0,24},{2,26},{4,28},{6,30},{8,0},{10,2},{12,4},{14,6},{16,8},{18,... | collective-permute-start | bytes 4718600 | tf_op jit(solution)/shard_map/ppermute | solution.py:14
  117.6 41.3 %collective-permute-start.21 = (s32[24]{0:T(128)S(1)}, s32[24]{0:T(128)S(1)}, u32[]{:S(2)}, u32[]{:S(2)}) collective-permute-start(s32[24]{0:T(128)S(1)} %broadcast_select_fusion.20), channel_id=1, source_target_pairs={{0,30},{2,0},{4,2},{6,4},{8,6},{10,8},{12,10},{14,12},{16,14},{18,... | collective-permute-start | bytes 296 | tf_op jit(solution)/shard_map/ppermute | solution.py:14
  122.0 76.6 %collective-permute-start.42 = (s32[16]{0:T(128)S(1)}, s32[16]{0:T(128)S(1)}, u32[]{:S(2)}, u32[]{:S(2)}) collective-permute-start(s32[16]{0:T(128)S(1)} %collective-permute-done.36), channel_id=1, source_target_pairs={{0,224},{32,0},{64,32},{96,64},{128,96},{160,128},{192,160},{224,1... | collective-permute-start | bytes 200 | tf_op jit(solution)/shard_map/ppermute | solution.py:14
  122.0 145.0 %collective-permute-start.47 = (s32[16]{0:T(128)S(1)}, s32[16]{0:T(128)S(1)}, u32[]{:S(2)}, u32[]{:S(2)}) collective-permute-start(s32[16]{0:T(128)S(1)} %collective-permute-done.41), channel_id=1, source_target_pairs={{0,224},{32,0},{64,32},{96,64},{128,96},{160,128},{192,160},{224,1... | collective-permute-start | bytes 200 | tf_op jit(solution)/shard_map/ppermute | solution.py:14
  164.4 38.8 %collective-permute-start.27 = (s32[24]{0:T(128)S(1)}, s32[24]{0:T(128)S(1)}, u32[]{:S(2)}, u32[]{:S(2)}) collective-permute-start(s32[24]{0:T(128)S(1)} %collective-permute-done.21), channel_id=1, source_target_pairs={{0,30},{2,0},{4,2},{6,4},{8,6},{10,8},{12,10},{14,12},{16,14},{18,... | collective-permute-start | bytes 296 | tf_op jit(solution)/shard_map/ppermute | solution.py:14
  193.5 73.0 %collective-permute-start.20 = (f32[24,128,128]{2,1,0:T(8,128)S(1)}, f32[24,128,128]{2,1,0:T(8,128)}, u32[]{:S(2)}, u32[]{:S(2)}) collective-permute-start(f32[24,128,128]{2,1,0:T(8,128)S(1)} %broadcast_select_fusion.2), channel_id=1, source_target_pairs={{0,16},{2,18},{4,20},{6,22},{8,24},{10,26},{12,28},{14,30},{16,0},... | collective-permute-start | bytes 4718600 | tf_op jit(solution)/shard_map/ppermute | solution.py:14
  203.2 110.6 %collective-permute-start.48 = (s32[16]{0:T(128)S(1)}, s32[16]{0:T(128)S(1)}, u32[]{:S(2)}, u32[]{:S(2)}) collective-permute-start(s32[16]{0:T(128)S(1)} %collective-permute-done.42), channel_id=1, source_target_pairs={{0,224},{32,0},{64,32},{96,64},{128,96},{160,128},{192,160},{224,1... | collective-permute-start | bytes 200 | tf_op jit(solution)/shard_map/ppermute | solution.py:14
  205.6 63.9 %collective-permute-start.33 = (s32[24]{0:T(128)S(1)}, s32[24]{0:T(128)S(1)}, u32[]{:S(2)}, u32[]{:S(2)}) collective-permute-start(s32[24]{0:T(128)S(1)} %collective-permute-done.27), channel_id=1, source_target_pairs={{0,30},{2,0},{4,2},{6,4},{8,6},{10,8},{12,10},{14,12},{16,14},{18,... | collective-permute-start | bytes 296 | tf_op jit(solution)/shard_map/ppermute | solution.py:14
  219.9 90.1 %collective-permute-start.16 = (f32[16,128,128]{2,1,0:T(8,128)}, f32[16,128,128]{2,1,0:T(8,128)}, u32[]{:S(2)}, u32[]{:S(2)}) collective-permute-start(f32[16,128,128]{2,1,0:T(8,128)} %broadcast_select_fusion.5), channel_id=1, source_target_pairs={{0,128},{32,160},{64,192},{96,224},{128,0},{160,32},{192,64},{224,... | collective-permute-start | bytes 3145736 | tf_op jit(solution)/shard_map/ppermute | solution.py:14
  266.7 53.2 %collective-permute-start.26 = (f32[24,128,128]{2,1,0:T(8,128)S(1)}, f32[24,128,128]{2,1,0:T(8,128)}, u32[]{:S(2)}, u32[]{:S(2)}) collective-permute-start(f32[24,128,128]{2,1,0:T(8,128)S(1)} %broadcast_select_fusion.3), channel_id=1, source_target_pairs={{0,30},{2,0},{4,2},{6,4},{8,6},{10,8},{12,10},{14,12},{16,14},{18,... | collective-permute-start | bytes 4718600 | tf_op jit(solution)/shard_map/ppermute | solution.py:14
  267.0 42.9 %collective-permute-start.40 = (s32[24]{0:T(128)S(1)}, s32[24]{0:T(128)S(1)}, u32[]{:S(2)}, u32[]{:S(2)}) collective-permute-start(s32[24]{0:T(128)S(1)} %collective-permute-done.34), channel_id=1, source_target_pairs={{0,30},{2,0},{4,2},{6,4},{8,6},{10,8},{12,10},{14,12},{16,14},{18,... | collective-permute-start | bytes 296 | tf_op jit(solution)/shard_map/ppermute | solution.py:14
  269.5 56.5 %collective-permute-start.53 = (s32[16]{0:T(128)S(1)}, s32[16]{0:T(128)S(1)}, u32[]{:S(2)}, u32[]{:S(2)}) collective-permute-start(s32[16]{0:T(128)S(1)} %collective-permute-done.47), channel_id=1, source_target_pairs={{0,224},{32,0},{64,32},{96,64},{128,96},{160,128},{192,160},{224,1... | collective-permute-start | bytes 200 | tf_op jit(solution)/shard_map/ppermute | solution.py:14
  314.5 48.1 %collective-permute-start.54 = (s32[16]{0:T(128)S(1)}, s32[16]{0:T(128)S(1)}, u32[]{:S(2)}, u32[]{:S(2)}) collective-permute-start(s32[16]{0:T(128)S(1)} %collective-permute-done.48), channel_id=1, source_target_pairs={{0,224},{32,0},{64,32},{96,64},{128,96},{160,128},{192,160},{224,1... | collective-permute-start | bytes 200 | tf_op jit(solution)/shard_map/ppermute | solution.py:14
  319.9 40.1 %collective-permute-start.32 = (f32[24,128,128]{2,1,0:T(8,128)}, f32[24,128,128]{2,1,0:T(8,128)}, u32[]{:S(2)}, u32[]{:S(2)}) collective-permute-start(f32[24,128,128]{2,1,0:T(8,128)} %collective-permute-done.26), channel_id=1, source_target_pairs={{0,30},{2,0},{4,2},{6,4},{8,6},{10,8},{12,10},{14,12},{16,14},{18,... | collective-permute-start | bytes 4718600 | tf_op jit(solution)/shard_map/ppermute | solution.py:14
  328.0 72.0 %collective-permute-start.59 = (s32[16]{0:T(128)S(1)}, s32[16]{0:T(128)S(1)}, u32[]{:S(2)}, u32[]{:S(2)}) collective-permute-start(s32[16]{0:T(128)S(1)} %collective-permute-done.53), channel_id=1, source_target_pairs={{0,224},{32,0},{64,32},{96,64},{128,96},{160,128},{192,160},{224,1... | collective-permute-start | bytes 200 | tf_op jit(solution)/shard_map/ppermute | solution.py:14
  359.9 46.9 %collective-permute-start.38 = (f32[24,128,128]{2,1,0:T(8,128)}, f32[24,128,128]{2,1,0:T(8,128)}, u32[]{:S(2)}, u32[]{:S(2)}) collective-permute-start(f32[24,128,128]{2,1,0:T(8,128)} %collective-permute-done.32), channel_id=1, source_target_pairs={{0,30},{2,0},{4,2},{6,4},{8,6},{10,8},{12,10},{14,12},{16,14},{18,... | collective-permute-start | bytes 4718600 | tf_op jit(solution)/shard_map/ppermute | solution.py:14
  406.8 40.0 %collective-permute-start.44 = (f32[24,128,128]{2,1,0:T(8,128)}, f32[24,128,128]{2,1,0:T(8,128)}, u32[]{:S(2)}, u32[]{:S(2)}) collective-permute-start(f32[24,128,128]{2,1,0:T(8,128)} %collective-permute-done.38), channel_id=1, source_target_pairs={{0,30},{2,0},{4,2},{6,4},{8,6},{10,8},{12,10},{14,12},{16,14},{18,... | collective-permute-start | bytes 4718600 | tf_op jit(solution)/shard_map/ppermute | solution.py:14
  446.8 44.5 %collective-permute-start.50 = (f32[24,128,128]{2,1,0:T(8,128)}, f32[24,128,128]{2,1,0:T(8,128)}, u32[]{:S(2)}, u32[]{:S(2)}) collective-permute-start(f32[24,128,128]{2,1,0:T(8,128)} %collective-permute-done.44), channel_id=1, source_target_pairs={{0,30},{2,0},{4,2},{6,4},{8,6},{10,8},{12,10},{14,12},{16,14},{18,... | collective-permute-start | bytes 4718600 | tf_op jit(solution)/shard_map/ppermute | solution.py:14
  491.3 38.3 %collective-permute-start.56 = (f32[24,128,128]{2,1,0:T(8,128)}, f32[24,128,128]{2,1,0:T(8,128)}, u32[]{:S(2)}, u32[]{:S(2)}) collective-permute-start(f32[24,128,128]{2,1,0:T(8,128)} %collective-permute-done.50), channel_id=1, source_target_pairs={{0,30},{2,0},{4,2},{6,4},{8,6},{10,8},{12,10},{14,12},{16,14},{18,... | collective-permute-start | bytes 4718600 | tf_op jit(solution)/shard_map/ppermute | solution.py:14
  529.6 41.1 %collective-permute-start.62 = (f32[24,128,128]{2,1,0:T(8,128)}, f32[24,128,128]{2,1,0:T(8,128)}, u32[]{:S(2)}, u32[]{:S(2)}) collective-permute-start(f32[24,128,128]{2,1,0:T(8,128)} %collective-permute-done.56), channel_id=1, source_target_pairs={{0,30},{2,0},{4,2},{6,4},{8,6},{10,8},{12,10},{14,12},{16,14},{18,... | collective-permute-start | bytes 4718600 | tf_op jit(solution)/shard_map/ppermute | solution.py:14
  (51 other events, 754.6 us)
Sparse Core Ops, SparseCore 0:
  593.7 71.2 all-reduce.1
where the time goes:
time: 686 us; the launch traced here: 676 us
  waiting for transfers between devices  318 us (46%)
  starting transfers between devices  155 us (23%)
  matrix products  138 us (20%)
  local copies, waits for them, and re-layouts  38.6 us (6%)
  between operations  14.2 us (2%)
  other arithmetic  12.6 us (2%)
    ppermute x63, waiting for transfers between devices, from_behind(): lax.ppermute(value, axis, [(i, (i + by) % size) for i in range(size)])  247 us
    ppermute x63, starting transfers between devices, from_behind(): lax.ppermute(value, axis, [(i, (i + by) % size) for i in range(size)])  155 us
    psum x1, waiting for transfers between devices, local(): summed = lax.psum(partial_value, 'depth')  71.4 us
    dot_general x8, matrix products, tile_product(): jnp.einsum('axy,amyz->amxz', row_tiles, gathered, precision=PRECISE)  64.9 us
    dot_general x8, matrix products, tile_product(): jnp.einsum('cam,amxz->cxz', routing.astype(jnp.float32), products, precis...  38.8 us
    dot_general x8, matrix products, tile_product(): jnp.einsum('amb,bxy->amxy', one_hot, col_tiles, precision=PRECISE)  34.6 us
    dot_general x8, local copies, waits for them, and re-layouts, tile_product(): jnp.einsum('axy,amyz->amxz', row_tiles, gathered, precision=PRECISE)  28.6 us
  transfers between devices with their start and end apart: 64, of which 21 were waited for; matrix products, arithmetic and copies ran while one was open for 24% of the time, Pallas kernels for 0%

commit v1 on v0

v1 whole, which is shorter than its diff:
```python
import functools

import jax
import jax.numpy as jnp
from jax import lax
from jax.experimental import pallas as pl
from jax.experimental.pallas import tpu as pltpu
from jax.sharding import PartitionSpec as P

MESH = pl.DeviceIdType.MESH
NZ, NY = 8, 4
ASLOT, BSLOT, CSLOT, BLK = 24, 8, 32, 128
ROWS = BLK // 2
PARTS, PSLOT = 4, ASLOT // 4
CCH, CSZ = 4, CSLOT // 4
LANE_A = 32
ZERO = 2 * ASLOT


def kernel(
    idx_ref, a_ref, b_ref, o_ref,
    idx_a, idx_b, idx_c, tab_v, low_v, tab_s, low_s,
    abuf, bbuf, bhi, blo, prods, acc, crecv,
    s_ia, r_ia, s_ib, r_ib, s_ic, r_ic, s_tab,
    s_al, s_ar, r_a, s_loc, s_bd, s_bf, s_bx, r_b, s_c, r_c, s_o, s_m, r_m,
):
    r = lax.axis_index("row")
    c = lax.axis_index("col")
    d = lax.axis_index("depth")
    y, q = r // 2, r % 2
    z, h = c // 2, c % 2
    half = (h + d) % 2
    own = q == h
    b_col = z * 2 + q
    b_depth = (d + h + q) % 2
    partner = (r, z * 2 + 1 - h, 1 - d)
    mate = (r, c, 1 - d)
    twin = (y * 2 + 1 - q, c, d)
    up, down = (((y + 1) % NY) * 2 + q, c, d), (((y + 3) % NY) * 2 + q, c, d)
    right, left = (r, ((z + 1) % NZ) * 2 + h, d), (r, ((z + 7) % NZ) * 2 + h, d)

    def remote(src, dst, send, recv, device):
        return pltpu.make_async_remote_copy(
            src_ref=src, dst_ref=dst, send_sem=send, recv_sem=recv, device_id=device, device_id_type=MESH
        )

    def landed(ref, sem):
        pltpu.make_async_copy(ref, ref, sem).wait()

    barrier = pltpu.get_barrier_semaphore()

    def greet(device):
        pl.semaphore_signal(barrier, inc=1, device_id=device, device_id_type=MESH)

    def greet_z(i, carry):
        greet((r, ((z + i) % NZ) * 2 + h, d))
        return carry

    lax.fori_loop(1, NZ, greet_z, 0)

    def greet_b(i, carry):
        yy = (y + i) % NY
        greet((yy * 2 + h, z * 2 + 1 - h, 1 - d))

        @pl.when(jnp.logical_not(own & (i == 0)))
        def _():
            greet((yy * 2 + h, c, d))

        return carry

    lax.fori_loop(0, NY, greet_b, 0)
    for device in (partner, mate, twin, up, down):
        greet(device)
    pl.semaphore_wait(barrier, NZ - 1 + 2 * NY + 5 - own.astype(jnp.int32))

    def send_ia(i):
        return remote(idx_ref, idx_a.at[z], s_ia.at[i], r_ia.at[z], (r, ((z + i) % NZ) * 2 + h, d))

    def send_ib(i):
        yy, core = (y + i // 2) % NY, i % 2
        return remote(idx_ref, idx_b.at[h * NY + y], s_ib.at[i], r_ib.at[h * NY + y], (yy * 2 + core, b_col, b_depth))

    def other_ib(i):
        return jnp.logical_not(own & (i // 2 == 0) & (i % 2 == q))

    send_ic = remote(idx_ref, idx_c, s_ic, r_ic, partner)

    def start_ia(i, carry):
        send_ia(i).start()
        return carry

    def start_ib(i, carry):
        pl.when(other_ib(i))(lambda: send_ib(i).start())
        return carry

    lax.fori_loop(1, NZ, start_ia, 0)
    lax.fori_loop(0, 2 * NY, start_ib, 0)
    send_ic.start()

    def send_bd(i, s):
        yy = (y + i) % NY
        return remote(
            b_ref.at[s, :, 0], bbuf.at[h, s * NY + y], s_bd.at[i, s], r_b.at[h, s * NY + y], (yy * 2 + s, b_col, b_depth)
        )

    local_b = pltpu.make_async_copy(b_ref.at[q, :, 0], bbuf.at[h, q * NY + y], r_b.at[h, q * NY + y])
    for i in (0, 1, 3):
        for s in (0, 1):
            if i:
                send_bd(i, s).start()
            else:
                pl.when(jnp.logical_not(own & (q == s)))(lambda: send_bd(0, s).start())
    pl.when(own)(local_b.start)

    def own_part(p):
        return a_ref.at[pl.ds(p * PSLOT, PSLOT), 0, pl.ds(half * ROWS, ROWS), :]

    def part(zz, p):
        return abuf.at[zz, pl.ds(p * PSLOT, PSLOT)]

    def a_right(dist, p):
        zz = (z + NZ - dist) % NZ
        return remote(part(zz, p), part(zz, p), s_ar.at[dist, p], r_a.at[zz, p], right)

    def a_left(dist, p):
        zz = (z + dist) % NZ
        return remote(part(zz, p), part(zz, p), s_al.at[dist, p], r_a.at[zz, p], left)

    local_a = pltpu.make_async_copy(a_ref.at[:, 0, pl.ds(half * ROWS, ROWS), :], abuf.at[z], s_loc)

    def start_a(p, carry):
        remote(own_part(p), part(z, p), s_ar.at[0, p], r_a.at[z, p], right).start()
        remote(own_part(p), part(z, p), s_al.at[0, p], r_a.at[z, p], left).start()
        return carry

    lax.fori_loop(0, PARTS, start_a, 0)
    local_a.start()

    idx_a[z] = idx_ref[...]

    @pl.when(own)
    def _():
        idx_b[h * NY + y] = idx_ref[...]

    acc[...] = jnp.zeros_like(acc)
    prods[0, ZERO] = jnp.zeros((ROWS, BLK), jnp.float32)
    prods[1, ZERO] = jnp.zeros((ROWS, BLK), jnp.float32)

    def wait_ia(i, carry):
        zz = (z + i) % NZ
        landed(idx_a.at[zz], r_ia.at[zz])
        return carry

    lax.fori_loop(1, NZ, wait_ia, 0)

    def wait_ib(i, carry):
        yy = (y + i) % NY
        landed(idx_b.at[(1 - h) * NY + yy], r_ib.at[(1 - h) * NY + yy])
        pl.when(jnp.logical_not(own & (i == 0)))(lambda: landed(idx_b.at[h * NY + yy], r_ib.at[h * NY + yy]))
        return carry

    lax.fori_loop(0, NY, wait_ib, 0)
    landed(idx_c, r_ic)

    a_all = jnp.sum(idx_a[...], axis=0)
    b_all = jnp.sum(idx_b[...], axis=0)
    a_row, a_in = a_all[0:1], a_all[1:2]
    b_key, b_to = b_all[2:3, :BLK], b_all[3:4, :BLK]

    def column(row, count):
        wide = jnp.broadcast_to(row, (count, BLK))
        at = lax.broadcasted_iota(jnp.int32, (count, BLK), 0)
        lane = lax.broadcasted_iota(jnp.int32, (count, BLK), 1)
        return jnp.sum(jnp.where(at == lane, wide, 0), axis=1, keepdims=True)

    key_col = column(b_key, BLK)
    at = lax.broadcasted_iota(jnp.int32, (BLK, 2 * BLK), 0)
    match = (key_col == a_in) & (a_in > 0)
    low_v[...] = jnp.zeros_like(low_v)
    for cp in (0, 1):
        mine = match & (at // (BLK // 2) == cp)
        first = jnp.min(jnp.where(mine, at % BSLOT, BSLOT), axis=0, keepdims=True)
        last = jnp.max(jnp.where(mine, at % BSLOT, 0), axis=0, keepdims=True)
        low_v[2 * cp : 2 * cp + 1] = jnp.where(first == BSLOT, 0, first)
        low_v[2 * cp + 1 : 2 * cp + 2] = last
    at2 = at[:, :BLK]
    lane2 = lax.broadcasted_iota(jnp.int32, (BLK, BLK), 1)
    earlier = (key_col == b_key) & (at2 < lane2) & (at2 // (BLK // 2) == lane2 // (BLK // 2))
    second = jnp.max(jnp.where(earlier, 1, 0), axis=0, keepdims=True)
    row_col = jnp.concatenate([column(a_row[:, :BLK], BLK), column(a_row[:, BLK:], BLK)], axis=0)
    in_col = jnp.concatenate([column(a_in[:, :BLK], BLK), column(a_in[:, BLK:], BLK)], axis=0)
    slot = lax.broadcasted_iota(jnp.int32, (2 * BLK, BLK), 0) % LANE_A
    weight = jnp.where((in_col == b_key) & (in_col > 0), slot + 1, 0)
    mine_c, other_c = idx_ref[...], idx_c[...]
    lane3 = lax.broadcasted_iota(jnp.int32, (CSLOT, BLK), 1)
    low_half = lane3 < BLK // 2
    at_zero = jnp.where(h == 0, mine_c, other_c)
    at_one = jnp.where(h == 0, other_c, mine_c)
    tab_v[0] = jnp.where(low_half, column(at_zero[4:5, :BLK], CSLOT), column(at_one[4:5, :BLK], CSLOT))
    tab_v[1] = jnp.where(low_half, column(at_zero[5:6, :BLK], CSLOT), column(at_one[5:6, :BLK], CSLOT))

    def one_slot(s, carry):
        out_row, out_col = tab_v[0, pl.ds(s, 1)], tab_v[1, pl.ds(s, 1)]
        found = jnp.max(jnp.where(row_col == out_row, weight, 0), axis=0, keepdims=True)
        place = jnp.clip(2 * found - 2 + second, 0, ZERO)
        tab_v[2, pl.ds(s, 1)] = jnp.where((found > 0) & (out_col == b_to), place, ZERO)
        return carry

    lax.fori_loop(0, CSLOT, one_slot, 0)
    tab_copy = pltpu.make_async_copy(tab_v.at[2], tab_s, s_tab.at[0])
    low_copy = pltpu.make_async_copy(low_v, low_s, s_tab.at[1])
    tab_copy.start()
    low_copy.start()
    tab_copy.wait()
    low_copy.wait()

    def spread(cp, zz, slot):
        return remote(bbuf.at[cp, zz], bbuf.at[cp, zz], s_bx.at[slot], r_b.at[cp, zz], twin)

    def split_b(cp, zz):
        def one(i, carry):
            value = bbuf[cp, zz, i]
            high = value.astype(jnp.bfloat16)
            bhi[cp, zz, i] = high
            blo[cp, zz, i] = (value - high.astype(jnp.float32)).astype(jnp.bfloat16)
            return carry

        lax.fori_loop(0, BSLOT, one, 0)

    def b_here(i, cp):
        zz = q * NY + (y + i) % NY
        landed(bbuf.at[cp, zz], r_b.at[cp, zz])
        spread(cp, zz, i * 2 + cp).start()

    def b_pass(cp):
        zz = q * NY + (y + (3 if cp == 0 else 1)) % NY
        return remote(bbuf.at[cp, zz], bbuf.at[cp, zz], s_bf.at[cp], r_b.at[cp, zz], up if cp == 0 else down)

    def a_step(dist):
        def one(p, carry):
            landed(part((z + NZ - dist) % NZ, p), r_a.at[(z + NZ - dist) % NZ, p])
            a_right(dist, p).start()
            landed(part((z + dist) % NZ, p), r_a.at[(z + dist) % NZ, p])
            a_left(dist, p).start()
            return carry

        lax.fori_loop(0, PARTS, one, 0)

    b_here(0, 0)
    b_here(0, 1)
    a_step(1)
    b_here(3, 0)
    b_pass(0).start()
    b_here(1, 1)
    b_pass(1).start()
    b_here(3, 1)
    b_here(1, 0)
    a_step(2)
    b_here(2, 0)
    b_here(2, 1)

    def take_b(i, carry):
        cp, zz = i // NZ, i % NZ

        @pl.when(zz // NY != q)
        def _():
            landed(bbuf.at[cp, zz], r_b.at[cp, zz])

        split_b(cp, zz)
        return carry

    lax.fori_loop(0, 2 * NZ, take_b, 0)
    local_a.wait()

    def group(k, carry):
        step = (k + 1) // 2
        zz = (z + NZ + jnp.where(k % 2 == 1, step, -step)) % NZ
        far_l, far_r = (z + NZ - 3) % NZ, (z + 3) % NZ

        @pl.when(k < PARTS)
        def _():
            landed(part(far_l, k), r_a.at[far_l, k])
            pl.when(k < PARTS // 2)(lambda: a_right(3, k).start())
            landed(part(far_r, k), r_a.at[far_r, k])
            pl.when(k >= PARTS // 2)(lambda: a_left(3, k).start())

        @pl.when(k == NZ - 1)
        def _():
            for p in range(PARTS):
                landed(part(zz, p), r_a.at[zz, p])

        def multiply(a, carry):
            value = abuf[zz, a]
            high = value.astype(jnp.bfloat16)
            low = (value - high.astype(jnp.float32)).astype(jnp.bfloat16)
            both = jnp.concatenate([high, low], axis=0)
            for o in (0, 1):
                cp = h if o == 0 else 1 - h
                b0 = low_s[2 * cp, zz * LANE_A + a]
                b1 = low_s[2 * cp + 1, zz * LANE_A + a]
                wide = jnp.concatenate([bhi[cp, zz, b0], bhi[cp, zz, b1]], axis=1)
                fine = jnp.concatenate([blo[cp, zz, b0], blo[cp, zz, b1]], axis=1)
                big = jnp.dot(both, wide, preferred_element_type=jnp.float32)
                small = jnp.dot(high, fine, preferred_element_type=jnp.float32)
                total = big[:ROWS] + (big[ROWS:] + small)
                prods[o, 2 * a] = total[:, :BLK]
                prods[o, 2 * a + 1] = total[:, BLK:]
            return carry

        lax.fori_loop(0, ASLOT, multiply, 0)

        def gather(s, carry):
            for o in (0, 1):
                cp = h if o == 0 else 1 - h
                base = cp * (BLK // 2) + zz * BSLOT
                terms = [prods[o, tab_s[s, base + b]] for b in range(BSLOT)]
                while len(terms) > 1:
                    terms = [x + w for x, w in zip(terms[::2], terms[1::2])]
                acc[o, s] += terms[0]
            return carry

        lax.fori_loop(0, CSLOT, gather, 0)
        return carry

    lax.fori_loop(0, NZ, group, 0)

    def c_piece(o, j):
        return acc.at[o, pl.ds(j * CSZ, CSZ)]

    def send_c(j):
        return remote(c_piece(1, j), crecv.at[pl.ds(j * CSZ, CSZ)], s_c.at[j], r_c.at[j], partner)

    def out_piece(j, which):
        return o_ref.at[pl.ds(j * CSZ, CSZ), 0, pl.ds(which * ROWS, ROWS), :]

    def send_m(j):
        return remote(c_piece(0, j), out_piece(j, half), s_m.at[j], r_m.at[j], mate)

    def store_o(j):
        return pltpu.make_async_copy(c_piece(0, j), out_piece(j, half), s_o.at[j])

    for j in range(CCH):
        send_c(j).start()
    for j in range(CCH):
        landed(crecv.at[pl.ds(j * CSZ, CSZ)], r_c.at[j])

        def add(s, carry):
            acc[0, s] += crecv[s]
            return carry

        lax.fori_loop(j * CSZ, (j + 1) * CSZ, add, 0)
        send_m(j).start()
        store_o(j).start()

    for j in range(CCH):
        landed(out_piece(j, 1 - half), r_m.at[j])
        store_o(j).wait()
        send_m(j).wait_send()
        send_c(j).wait_send()

    def end_ia(i, carry):
        send_ia(i).wait_send()
        return carry

    def end_ib(i, carry):
        pl.when(other_ib(i))(lambda: send_ib(i).wait_send())
        return carry

    lax.fori_loop(1, NZ, end_ia, 0)
    lax.fori_loop(0, 2 * NY, end_ib, 0)
    send_ic.wait_send()
    for i in (0, 1, 3):
        for s in (0, 1):
            if i:
                send_bd(i, s).wait_send()
            else:
                pl.when(jnp.logical_not(own & (q == s)))(lambda: send_bd(0, s).wait_send())
    for cp in (0, 1):
        b_pass(cp).wait_send()
        for i in range(NY):
            spread(cp, q * NY + (y + i) % NY, i * 2 + cp).wait_send()

    def end_a(p, carry):
        for dist in range(3):
            a_right(dist, p).wait_send()
            a_left(dist, p).wait_send()
        pl.when(p < PARTS // 2)(lambda: a_right(3, p).wait_send())
        pl.when(p >= PARTS // 2)(lambda: a_left(3, p).wait_send())
        return carry

    lax.fori_loop(0, PARTS, end_a, 0)


def index_rows(a_index, b_index, c_index):
    y = lax.axis_index("row") // 2
    z, h = lax.axis_index("col") // 2, lax.axis_index("col") % 2
    wide = jnp.zeros((8, 2 * BLK), jnp.int32)
    wide = lax.dynamic_update_slice(wide, a_index[:, :, 0] + 1, (0, z * LANE_A))
    for s in (0, 1):
        wide = lax.dynamic_update_slice(wide, b_index[:, s, :, 0] + 1, (2, h * (BLK // 2) + (s * NY + y) * BSLOT))
    return lax.dynamic_update_slice(wide, c_index[:, :, 0] + 1, (4, 0))


def local(a_blocks, a_index, b_blocks, b_index, c_index):
    dma = pltpu.SemaphoreType.DMA
    f32, bf16, i32 = jnp.float32, jnp.bfloat16, jnp.int32
    anywhere = pl.BlockSpec(memory_space=pl.ANY)
    return pl.pallas_call(
        kernel,
        out_shape=jax.ShapeDtypeStruct((CSLOT, 1, BLK, BLK), f32),
        in_specs=[pl.BlockSpec(memory_space=pltpu.VMEM), anywhere, anywhere],
        out_specs=anywhere,
        scratch_shapes=[
            pltpu.VMEM((NZ, 8, 2 * BLK), i32),
            pltpu.VMEM((2 * NY, 8, 2 * BLK), i32),
            pltpu.VMEM((8, 2 * BLK), i32),
            pltpu.VMEM((3, CSLOT, BLK), i32),
            pltpu.VMEM((8, 2 * BLK), i32),
            pltpu.SMEM((CSLOT, BLK), i32),
            pltpu.SMEM((8, 2 * BLK), i32),
            pltpu.VMEM((NZ, ASLOT, ROWS, BLK), f32),
            pltpu.VMEM((2, NZ, BSLOT, BLK, BLK), f32),
            pltpu.VMEM((2, NZ, BSLOT, BLK, BLK), bf16),
            pltpu.VMEM((2, NZ, BSLOT, BLK, BLK), bf16),
            pltpu.VMEM((2, ZERO + 1, ROWS, BLK), f32),
            pltpu.VMEM((2, CSLOT, ROWS, BLK), f32),
            pltpu.VMEM((CSLOT, ROWS, BLK), f32),
            dma((NZ,)), dma((NZ,)), dma((2 * NY,)), dma((2 * NY,)), dma, dma, dma((2,)),
            dma((4, PARTS)), dma((4, PARTS)), dma((NZ, PARTS)), dma,
            dma((NY, 2)), dma((2,)), dma((2 * NY,)), dma((2, NZ)),
            dma((CCH,)), dma((CCH,)), dma((CCH,)), dma((CCH,)), dma((CCH,)),
        ],
        compiler_params=pltpu.CompilerParams(
            collective_id=0, has_side_effects=True, vmem_limit_bytes=56 * 1024 * 1024
        ),
        cost_estimate=pl.CostEstimate(flops=10**10, bytes_accessed=10**7, transcendentals=0),
    )(index_rows(a_index, b_index, c_index), a_blocks, b_blocks)


def solution(mesh):
    in_specs = (
        P("row", "col", None, None),
        P(None, "row", "col"),
        P(None, "row", "col", None, None),
        P(None, None, "row", "col"),
        P(None, "row", "col"),
    )
    out_specs = P("row", "col", None, None)
    return jax.shard_map(local, mesh=mesh, in_specs=in_specs, out_specs=out_specs, check_vma=False)
```

time: 686 us -> 157 us (0.23)
  the two profiles are of different devices: /device:TPU:1 before, /device:TPU:12 now
where the time goes in v1:
time: 157 us; the launch traced here: 156 us
  Pallas kernels  149 us (95%)
  local copies, waits for them, and re-layouts  5.53 us (4%)
  other arithmetic  2.06 us (1%)
    pallas_call x1, Pallas kernels, local(): pl.pallas_call(kernel, out_shape=jax.ShapeDtypeStruct((CSLOT, 1, BLK, BLK...  149 us
    unnamed x3, local copies, waits for them, and re-layouts  3.73 us

profile of v1, /device:TPU:12, one launch (start us, length us, event | category | flops | bytes accessed | tf_op | source)
XLA Modules:
  0.0 156.4 jit_solution(3482481266414644911)
XLA Ops:
  0.0 0.7 broadcast_add_fusion.1
  0.7 0.7 broadcast_add_fusion
  1.4 0.7 slice_add_fusion
  2.1 0.3 dynamic_update_slice.12
  2.4 0.6 dynamic_update_slice.13
  2.9 0.6 dynamic_update_slice.14
  3.5 0.4 dynamic_update_slice.15.idx_ref
  3.9 0.0 copy-start
  3.9 0.6 copy-done
  4.5 148.8 %shard_map.55 = f32[32,1,128,128]{3,2,1,0:T(8,128)} custom-call(s32[8,256]{1,0:T(8,128)} %copy-done, f32[24,1,128,128]{3,2,1,0:T(8,128)} %a_ref.1, f32[2,8,1,128,128]{4,3,2,1,0:T(8,128)} %b_ref.1), custom_call_target="tpu_custom_call" | custom-call | flops 10000000000 | bytes 10000000 | tf_op jit(solution)/shard_map/pallas_call | solution.py:408
  153.3 3.1 %copy.11 = f32[32,1,128,128]{3,2,1,0:T(8,128)} copy(f32[32,1,128,128]{3,2,1,0:T(8,128)} %shard_map.55) | data formatting | bytes 4194304
  (1 shorter events, 0.0 us)
Async XLA Ops:
  3.9 0.6 copy-start

commit v2 on v0

v2 whole, which is shorter than its diff:
```python
import functools

import jax
import jax.numpy as jnp
from jax import lax
from jax.experimental import pallas as pl
from jax.experimental.pallas import tpu as pltpu
from jax.sharding import PartitionSpec as P

MESH = pl.DeviceIdType.MESH
NZ, NY = 8, 4
ASLOT, BSLOT, CSLOT, BLK = 24, 8, 32, 128
ROWS = BLK // 2
PARTS, PROW = 4, ROWS // 4
SPANS, SROW = 2, ROWS // 2
CCH, CSZ = 4, CSLOT // 4
LANE_A = 32
ZERO = 2 * ASLOT


def kernel(
    idx_ref, a_ref, b_ref, o_ref,
    idx_a, idx_b, idx_c, tab_v, low_v, tab_s, low_s,
    abuf, bbuf, bhi, blo, prods, acc, crecv,
    s_ia, r_ia, s_ib, r_ib, s_ic, r_ic, s_tab,
    s_al, s_ar, r_a, s_loc, s_bd, s_bn, s_bf, s_bx, r_b, s_c, r_c, s_o, s_m, r_m,
):
    r = lax.axis_index("row")
    c = lax.axis_index("col")
    d = lax.axis_index("depth")
    y, q = r // 2, r % 2
    z, h = c // 2, c % 2
    half = (h + d) % 2
    own = q == h
    role = (q + h) % 2
    b_col = z * 2 + q
    b_depth = (d + h + q) % 2
    partner = (r, z * 2 + 1 - h, 1 - d)
    mate = (r, c, 1 - d)
    twin = (y * 2 + 1 - q, c, d)
    up, down = (((y + 1) % NY) * 2 + q, c, d), (((y + 3) % NY) * 2 + q, c, d)
    right, left = (r, ((z + 1) % NZ) * 2 + h, d), (r, ((z + 7) % NZ) * 2 + h, d)

    def remote(src, dst, send, recv, device):
        return pltpu.make_async_remote_copy(
            src_ref=src, dst_ref=dst, send_sem=send, recv_sem=recv, device_id=device, device_id_type=MESH
        )

    def landed(ref, sem):
        pltpu.make_async_copy(ref, ref, sem).wait()

    barrier = pltpu.get_barrier_semaphore()

    def greet(device):
        pl.semaphore_signal(barrier, inc=1, device_id=device, device_id_type=MESH)

    def greet_z(i, carry):
        greet((r, ((z + i) % NZ) * 2 + h, d))
        return carry

    lax.fori_loop(1, NZ, greet_z, 0)

    def greet_b(i, carry):
        yy = (y + i) % NY
        greet((yy * 2 + h, z * 2 + 1 - h, 1 - d))

        @pl.when(jnp.logical_not(own & (i == 0)))
        def _():
            greet((yy * 2 + h, c, d))

        return carry

    lax.fori_loop(0, NY, greet_b, 0)
    for device in (partner, mate, twin, up, down):
        greet(device)
    pl.semaphore_wait(barrier, NZ - 1 + 2 * NY + 5 - own.astype(jnp.int32))

    def send_bd(i, s):
        yy = (y + i) % NY
        return remote(b_ref.at[s, :, 0], bbuf.at[0, s * NY + y], s_bd.at[i, s], r_b.at[0, s * NY + y], (yy * 2 + s, c, d))

    def send_bp(s):
        return remote(
            b_ref.at[s, :, 0], bbuf.at[1, s * NY + y], s_bd.at[0, s], r_b.at[1, s * NY + y],
            (y * 2 + s, z * 2 + 1 - h, 1 - d),
        )

    local_b = pltpu.make_async_copy(b_ref.at[q, :, 0], bbuf.at[0, q * NY + y], r_b.at[0, q * NY + y])

    @pl.when(own)
    def _():
        for s in (0, 1):
            pl.when(q != s)(lambda: send_bd(0, s).start())
            send_bd(1, s).start()
            send_bd(3, s).start()
        local_b.start()

    @pl.when(jnp.logical_not(own))
    def _():
        send_bp(0).start()
        send_bp(1).start()

    def own_part(p):
        return a_ref.at[:, 0, pl.ds(half * ROWS + p * PROW, PROW), :]

    def part(zz, p):
        return abuf.at[zz, p]

    def turn(j):
        return j + 1 - 2 * (j % 2)

    def a_right(dist, j):
        zz = (z + NZ - dist) % NZ
        return remote(part(zz, j), part(zz, j), s_ar.at[dist, j], r_a.at[zz, j], right)

    def a_left(dist, j):
        zz, p = (z + dist) % NZ, turn(j)
        return remote(part(zz, p), part(zz, p), s_al.at[dist, j], r_a.at[zz, p], left)

    def from_left(dist, j):
        zz = (z + NZ - dist) % NZ
        landed(part(zz, j), r_a.at[zz, j])

    def from_right(dist, j):
        zz, p = (z + dist) % NZ, turn(j)
        landed(part(zz, p), r_a.at[zz, p])

    def local_a(p):
        return pltpu.make_async_copy(own_part(p), part(z, p), s_loc.at[p])

    def start_a(j, carry):
        p = turn(j)
        remote(own_part(j), part(z, j), s_ar.at[0, j], r_a.at[z, j], right).start()
        remote(own_part(p), part(z, p), s_al.at[0, j], r_a.at[z, p], left).start()
        local_a(j).start()
        return carry

    lax.fori_loop(0, PARTS, start_a, 0)

    def send_ia(i):
        return remote(idx_ref, idx_a.at[z], s_ia.at[i], r_ia.at[z], (r, ((z + i) % NZ) * 2 + h, d))

    def send_ib(i):
        yy, core = (y + i // 2) % NY, i % 2
        at = role * NY + y
        return remote(idx_ref, idx_b.at[at], s_ib.at[i], r_ib.at[at], (yy * 2 + core, b_col, b_depth))

    def other_ib(i):
        return jnp.logical_not(own & (i // 2 == 0) & (i % 2 == q))

    send_ic = remote(idx_ref, idx_c, s_ic, r_ic, partner)

    def start_ia(i, carry):
        send_ia(i).start()
        return carry

    def start_ib(i, carry):
        pl.when(other_ib(i))(lambda: send_ib(i).start())
        return carry

    lax.fori_loop(1, NZ, start_ia, 0)
    lax.fori_loop(0, 2 * NY, start_ib, 0)
    send_ic.start()
    idx_a[z] = idx_ref[...]

    @pl.when(own)
    def _():
        idx_b[y] = idx_ref[...]

    acc[...] = jnp.zeros_like(acc)
    for v in range(SPANS):
        for o in (0, 1):
            prods[v, o, ZERO] = jnp.zeros((SROW, BLK), jnp.float32)

    def tables():
        def wait_ia(i, carry):
            zz = (z + i) % NZ
            landed(idx_a.at[zz], r_ia.at[zz])
            return carry

        lax.fori_loop(1, NZ, wait_ia, 0)

        def wait_ib(i, carry):
            yy = (y + i) % NY
            landed(idx_b.at[NY + yy], r_ib.at[NY + yy])
            pl.when(jnp.logical_not(own & (i == 0)))(lambda: landed(idx_b.at[yy], r_ib.at[yy]))
            return carry

        lax.fori_loop(0, NY, wait_ib, 0)
        landed(idx_c, r_ic)

        a_sets = []
        for g in (0, 1):
            rolled = [pltpu.roll(idx_a[g * 4 + i] + 1, i * LANE_A, 1) if i else idx_a[g * 4] + 1 for i in range(4)]
            a_sets.append(rolled[0] + rolled[1] + (rolled[2] + rolled[3]))
        rolled = [pltpu.roll(idx_b[i] + 1, (i // NY) * (BLK // 2) + (i % NY) * BSLOT, 1) if i else idx_b[0] + 1 for i in range(2 * NY)]
        while len(rolled) > 1:
            rolled = [x + w for x, w in zip(rolled[::2], rolled[1::2])]
        b_key, b_to = rolled[0][2:3], rolled[0][3:4]
        a_in = jnp.concatenate([a_sets[0][1:2], a_sets[1][1:2]], axis=1)

        def column(row, count):
            wide = jnp.broadcast_to(row, (count, BLK))
            at = lax.broadcasted_iota(jnp.int32, (count, BLK), 0)
            lane = lax.broadcasted_iota(jnp.int32, (count, BLK), 1)
            return jnp.sum(jnp.where(at == lane, wide, 0), axis=1, keepdims=True)

        key_col = column(b_key, BLK)
        at = lax.broadcasted_iota(jnp.int32, (BLK, 2 * BLK), 0)
        match = (key_col == a_in) & (a_in > 0)
        low_v[...] = jnp.zeros_like(low_v)
        for o in (0, 1):
            mine = match & (at // (BLK // 2) == o)
            first = jnp.min(jnp.where(mine, at % BSLOT, BSLOT), axis=0, keepdims=True)
            last = jnp.max(jnp.where(mine, at % BSLOT, 0), axis=0, keepdims=True)
            low_v[2 * o : 2 * o + 1] = jnp.where(first == BSLOT, 0, first)
            low_v[2 * o + 1 : 2 * o + 2] = last
        at2 = at[:, :BLK]
        lane2 = lax.broadcasted_iota(jnp.int32, (BLK, BLK), 1)
        earlier = (key_col == b_key) & (at2 < lane2) & (at2 // (BLK // 2) == lane2 // (BLK // 2))
        second = jnp.max(jnp.where(earlier, 1, 0), axis=0, keepdims=True)
        row_col = jnp.concatenate([column(a_sets[g][0:1], BLK) for g in (0, 1)], axis=0)
        in_col = jnp.concatenate([column(a_sets[g][1:2], BLK) for g in (0, 1)], axis=0)
        slot = lax.broadcasted_iota(jnp.int32, (2 * BLK, BLK), 0) % LANE_A
        weight = jnp.where((in_col == b_key) & (in_col > 0), slot + 1, 0)
        lane3 = lax.broadcasted_iota(jnp.int32, (CSLOT, BLK), 1)
        mine_c, other_c = idx_ref[...] + 1, idx_c[...] + 1
        for i in (0, 1):
            tab_v[i] = jnp.where(
                lane3 < BLK // 2, column(mine_c[4 + i : 5 + i], CSLOT), column(other_c[4 + i : 5 + i], CSLOT)
            )

        def one_slot(s, carry):
            out_row, out_col = tab_v[0, pl.ds(s, 1)], tab_v[1, pl.ds(s, 1)]
            found = jnp.max(jnp.where(row_col == out_row, weight, 0), axis=0, keepdims=True)
            place = jnp.clip(2 * found - 2 + second, 0, ZERO)
            tab_v[2, pl.ds(s, 1)] = jnp.where((found > 0) & (out_col == b_to), place, ZERO)
            return carry

        lax.fori_loop(0, CSLOT, one_slot, 0)
        for copy in (tab_copy, low_copy):
            copy.start()

    tab_copy = pltpu.make_async_copy(tab_v.at[2], tab_s, s_tab.at[0])
    low_copy = pltpu.make_async_copy(low_v, low_s, s_tab.at[1])

    def spread(o, zz, slot):
        return remote(bbuf.at[o, zz], bbuf.at[o, zz], s_bx.at[slot], r_b.at[o, zz], twin)

    def split_b(o, zz):
        def one(i, carry):
            value = bbuf[o, zz, i]
            high = value.astype(jnp.bfloat16)
            bhi[o, zz, i] = high
            blo[o, zz, i] = (value - high.astype(jnp.float32)).astype(jnp.bfloat16)
            return carry

        lax.fori_loop(0, BSLOT, one, 0)

    def b_slot(i):
        return q * NY + (y + i) % NY

    def b_here(o, i):
        landed(bbuf.at[o, b_slot(i)], r_b.at[o, b_slot(i)])

    def b_next(way):
        zz = b_slot(0)
        return remote(bbuf.at[1, zz], bbuf.at[1, zz], s_bn.at[way], r_b.at[1, zz], (up, down)[way])

    def b_pass(o):
        zz = b_slot(3 if o == 0 else 1)
        return remote(bbuf.at[o, zz], bbuf.at[o, zz], s_bf.at[o], r_b.at[o, zz], (up, down)[o])

    def b_done(o, i):
        spread(o, b_slot(i), i * 2 + o).start()
        split_b(o, b_slot(i))

    def a_step(dist, j):
        from_left(dist, j)
        a_right(dist, j).start()
        from_right(dist, j)
        a_left(dist, j).start()

    a_step(1, 0)
    b_here(0, 0)
    b_done(0, 0)
    a_step(1, 1)
    b_here(1, 0)
    b_next(0).start()
    b_next(1).start()
    b_done(1, 0)
    a_step(1, 2)
    b_here(0, 3)
    b_pass(0).start()
    b_here(0, 1)
    b_done(0, 3)
    b_done(0, 1)
    a_step(1, 3)
    tables()
    b_here(1, 1)
    b_pass(1).start()
    b_here(1, 3)
    b_done(1, 1)
    b_done(1, 3)
    a_step(2, 0)
    b_here(0, 2)
    b_done(0, 2)
    a_step(2, 1)
    b_here(1, 2)
    b_done(1, 2)
    for j in (2, 3):
        from_left(2, j)
        from_right(2, j)
    a_step(3, 0)
    for j in (2, 3):
        a_right(2, j).start()
        a_left(2, j).start()

    def take_b(i, carry):
        o, zz = i // NY, (1 - q) * NY + i % NY
        landed(bbuf.at[o, zz], r_b.at[o, zz])
        split_b(o, zz)
        return carry

    lax.fori_loop(0, 2 * NY, take_b, 0)
    for p in range(PARTS):
        local_a(p).wait()
    tab_copy.wait()
    low_copy.wait()

    def multiply(zz, first, count):
        rows = count * PROW

        def one(a):
            value = abuf[zz, first : first + count, a].reshape(rows, BLK)
            high = value.astype(jnp.bfloat16)
            low = (value - high.astype(jnp.float32)).astype(jnp.bfloat16)
            both = jnp.concatenate([high, low], axis=0)
            for o in (0, 1):
                b0 = low_s[2 * o, zz * LANE_A + a]
                b1 = low_s[2 * o + 1, zz * LANE_A + a]
                wide = jnp.concatenate([bhi[o, zz, b0], bhi[o, zz, b1]], axis=1)
                fine = jnp.concatenate([blo[o, zz, b0], blo[o, zz, b1]], axis=1)
                big = jnp.dot(both, wide, preferred_element_type=jnp.float32)
                small = jnp.dot(high, fine, preferred_element_type=jnp.float32)
                total = big[:rows] + (big[rows:] + small)
                for v in range(rows // SROW):
                    span = first * PROW // SROW + v
                    prods[span, o, 2 * a] = total[v * SROW : (v + 1) * SROW, :BLK]
                    prods[span, o, 2 * a + 1] = total[v * SROW : (v + 1) * SROW, BLK:]

        def some(i, carry):
            for j in range(UNROLL):
                one(i * UNROLL + j)
            return carry

        lax.fori_loop(0, ASLOT // UNROLL, some, 0)

    def gather(zz, o, spans, begin, end):
        base = o * (BLK // 2) + zz * BSLOT

        def some(i, carry):
            for j in (0, 1):
                s = i * 2 + j
                at = [tab_s[s, base + b] for b in range(BSLOT)]
                for v in spans:
                    terms = [prods[v, o, p] for p in at]
                    while len(terms) > 1:
                        terms = [x + w for x, w in zip(terms[::2], terms[1::2])]
                    acc[v, o, s] += terms[0]
            return carry

        lax.fori_loop(begin // 2, end // 2, some, 0)

    def near(k, carry):
        step = (k + 1) // 2
        zz = (z + NZ + jnp.where(k % 2 == 1, step, -step)) % NZ
        multiply(zz, 0, PARTS)
        for o in (0, 1):
            gather(zz, o, range(SPANS), 0, CSLOT)
        return carry

    lax.fori_loop(0, 5, near, 0)

    def c_piece(v, o, j):
        return acc.at[v, o, pl.ds(j * CSZ, CSZ)]

    def c_landing(v, j):
        return crecv.at[v, pl.ds(j * CSZ, CSZ)]

    def send_c(v, j):
        return remote(c_piece(v, 1, j), c_landing(v, j), s_c.at[v, j], r_c.at[v, j], partner)

    def out_piece(v, j, which):
        return o_ref.at[pl.ds(j * CSZ, CSZ), 0, pl.ds(which * ROWS + v * SROW, SROW), :]

    def send_m(v, j):
        return remote(c_piece(v, 0, j), out_piece(v, j, half), s_m.at[v, j], r_m.at[v, j], mate)

    def store_o(v, j):
        return pltpu.make_async_copy(c_piece(v, 0, j), out_piece(v, j, half), s_o.at[v, j])

    far = ((z + 3) % NZ, (z + NZ - 3) % NZ)
    last = (z + 4) % NZ
    for v in range(SPANS):
        if v == 0:
            from_left(3, 2)
            a_right(3, 2).start()
            from_right(3, 2)
            a_left(3, 2).start()
        from_left(3, 2 * v + 1)
        from_right(3, 2 * v + 1)
        for zz in far:
            multiply(zz, 2 * v, 2)
            for o in (0, 1):
                gather(zz, o, (v,), 0, CSLOT)
        from_left(4, 2 * v)
        from_right(4, 2 * v)
        multiply(last, 2 * v, 2)
        for j in range(CCH):
            gather(last, 1, (v,), j * CSZ, (j + 1) * CSZ)
            send_c(v, j).start()
        gather(last, 0, (v,), 0, CSLOT)
    for v in range(SPANS):
        for j in range(CCH):
            landed(c_landing(v, j), r_c.at[v, j])

            def add(s, carry):
                acc[v, 0, s] += crecv[v, s]
                return carry

            lax.fori_loop(j * CSZ, (j + 1) * CSZ, add, 0)
            send_m(v, j).start()
            store_o(v, j).start()

    for v in range(SPANS):
        for j in range(CCH):
            landed(out_piece(v, j, 1 - half), r_m.at[v, j])
            store_o(v, j).wait()
            send_m(v, j).wait_send()
            send_c(v, j).wait_send()

    def end_ia(i, carry):
        send_ia(i).wait_send()
        return carry

    def end_ib(i, carry):
        pl.when(other_ib(i))(lambda: send_ib(i).wait_send())
        return carry

    lax.fori_loop(1, NZ, end_ia, 0)
    lax.fori_loop(0, 2 * NY, end_ib, 0)
    send_ic.wait_send()

    @pl.when(own)
    def _():
        for s in (0, 1):
            pl.when(q != s)(lambda: send_bd(0, s).wait_send())
            send_bd(1, s).wait_send()
            send_bd(3, s).wait_send()

    @pl.when(jnp.logical_not(own))
    def _():
        send_bp(0).wait_send()
        send_bp(1).wait_send()

    for o in (0, 1):
        b_next(o).wait_send()
        b_pass(o).wait_send()
        for i in range(NY):
            spread(o, b_slot(i), i * 2 + o).wait_send()

    def end_a(j, carry):
        for dist in range(3):
            a_right(dist, j).wait_send()
            a_left(dist, j).wait_send()

        @pl.when(j % 2 == 0)
        def _():
            a_right(3, j).wait_send()
            a_left(3, j).wait_send()

        return carry

    lax.fori_loop(0, PARTS, end_a, 0)


UNROLL = 4


def index_rows(a_index, b_index, c_index):
    def wide(part):
        return jnp.pad(part, ((0, 0), (0, BLK - part.shape[1])), constant_values=-1)

    b_rows = jnp.pad(b_index[..., 0], ((0, 0), (0, 0), (0, BLK // 4 - BSLOT)), constant_values=-1)
    rows = [a_index[:, :, 0], b_rows.reshape(2, BLK // 2), c_index[:, :, 0], jnp.full((2, BLK), -1, jnp.int32)]
    return jnp.concatenate([wide(part) for part in rows], axis=0)


def local(a_blocks, a_index, b_blocks, b_index, c_index):
    dma = pltpu.SemaphoreType.DMA
    f32, bf16, i32 = jnp.float32, jnp.bfloat16, jnp.int32
    anywhere = pl.BlockSpec(memory_space=pl.ANY)
    return pl.pallas_call(
        kernel,
        out_shape=jax.ShapeDtypeStruct((CSLOT, 1, BLK, BLK), f32),
        in_specs=[pl.BlockSpec(memory_space=pltpu.VMEM), anywhere, anywhere],
        out_specs=anywhere,
        scratch_shapes=[
            pltpu.VMEM((NZ, 8, BLK), i32),
            pltpu.VMEM((2 * NY, 8, BLK), i32),
            pltpu.VMEM((8, BLK), i32),
            pltpu.VMEM((3, CSLOT, BLK), i32),
            pltpu.VMEM((8, 2 * BLK), i32),
            pltpu.SMEM((CSLOT, BLK), i32),
            pltpu.SMEM((8, 2 * BLK), i32),
            pltpu.VMEM((NZ, PARTS, ASLOT, PROW, BLK), f32),
            pltpu.VMEM((2, NZ, BSLOT, BLK, BLK), f32),
            pltpu.VMEM((2, NZ, BSLOT, BLK, BLK), bf16),
            pltpu.VMEM((2, NZ, BSLOT, BLK, BLK), bf16),
            pltpu.VMEM((SPANS, 2, ZERO + 1, SROW, BLK), f32),
            pltpu.VMEM((SPANS, 2, CSLOT, SROW, BLK), f32),
            pltpu.VMEM((SPANS, CSLOT, SROW, BLK), f32),
            dma((NZ,)), dma((NZ,)), dma((2 * NY,)), dma((2 * NY,)), dma, dma, dma((2,)),
            dma((4, PARTS)), dma((4, PARTS)), dma((NZ, PARTS)), dma((PARTS,)),
            dma((NY, 2)), dma((2,)), dma((2,)), dma((2 * NY,)), dma((2, NZ)),
            dma((SPANS, CCH)), dma((SPANS, CCH)), dma((SPANS, CCH)), dma((SPANS, CCH)), dma((SPANS, CCH)),
        ],
        compiler_params=pltpu.CompilerParams(
            collective_id=0, has_side_effects=True, vmem_limit_bytes=56 * 1024 * 1024
        ),
        cost_estimate=pl.CostEstimate(flops=10**10, bytes_accessed=10**7, transcendentals=0),
    )(index_rows(a_index, b_index, c_index), a_blocks, b_blocks)


def solution(mesh):
    in_specs = (
        P("row", "col", None, None),
        P(None, "row", "col"),
        P(None, "row", "col", None, None),
        P(None, None, "row", "col"),
        P(None, "row", "col"),
    )
    out_specs = P("row", "col", None, None)
    return jax.shard_map(local, mesh=mesh, in_specs=in_specs, out_specs=out_specs, check_vma=False)
```

time: 686 us -> 124 us (0.18); the launches traced: 676 us -> 124 us
  waiting for transfers between devices: 318 us -> 0 us
  starting transfers between devices: 155 us -> 0 us
  matrix products: 138 us -> 0 us
  Pallas kernels: 0 us -> 118 us
  local copies, waits for them, and re-layouts: 38.6 us -> 3.98 us
  between operations: 14.2 us -> 0.01 us
  other arithmetic: 12.6 us -> 1.36 us
    ppermute x63 -> x0, waiting for transfers between devices: 247 us -> none  [from_behind(): lax.ppermute(value, axis, [(i, (i + by) % size) for i in range(size)])]
    ppermute x63 -> x0, starting transfers between devices: 155 us -> none  [from_behind(): lax.ppermute(value, axis, [(i, (i + by) % size) for i in range(size)])]
    dot_general x24 -> x0, matrix products: 138 us -> none  [the longest x8 64.9 us: tile_product(): jnp.einsum('axy,amyz->amxz', row_tiles, gathered, precision=PRECISE)]
    pallas_call x0 -> x1, Pallas kernels: none -> 118 us  [local(): pl.pallas_call(kernel, out_shape=jax.ShapeDtypeStruct((CSLOT, 1, BLK, BLK...]
    psum x1 -> x0, waiting for transfers between devices: 71.4 us -> none  [local(): summed = lax.psum(partial_value, 'depth')]
    dot_general x8 -> x0, local copies, waits for them, and re-layouts: 28.6 us -> none  [tile_product(): jnp.einsum('axy,amyz->amxz', row_tiles, gathered, precision=PRECISE)]
    select_n x19 -> x0, other arithmetic: 8.84 us -> none  [keep_where(): jnp.where(chosen, fresh_part, held_part)]
  transfers between devices with their start and end apart: 64 -> 0, of which waited for: 21 -> 0; matrix products, arithmetic and copies ran while one was open for 24% -> 0% of each run, Pallas kernels for 0% -> 0%
where the time goes in v2:
time: 124 us
  Pallas kernels  118 us (95%)
  local copies, waits for them, and re-layouts  3.98 us (3%)
  other arithmetic  1.36 us (1%)
    pallas_call x1, Pallas kernels, local(): pl.pallas_call(kernel, out_shape=jax.ShapeDtypeStruct((CSLOT, 1, BLK, BLK...  118 us
    unnamed x1, local copies, waits for them, and re-layouts  3.14 us

profile of v2, /device:TPU:1, one launch (start us, length us, event | category | flops | bytes accessed | tf_op | source)
XLA Modules:
  0.0 123.6 jit_solution(1589036572378804666)
XLA Ops:
  0.0 0.1 pad.23.clone
  0.1 0.7 pad.17
  0.8 0.1 reshape.3
  0.9 1.4 %fusion.idx_ref = s32[8,128]{1,0:T(8,128)} fusion(s32[2,32]{1,0:T(2,128)} %bitcast.4, s32[2,64]{1,0:T(2,128)S(1)} %reshape.3, s32[2,24]{1,0:T(2,128)} %bitcast.5, s32[8]{0:T(128)S(1)} %pad.23.clone), kind=kLoop, calls=%fused_computation.5 | loop fusion | flops 13312 | bytes 5088 | tf_op jit(solution)/shard_map/concatenate | solution.py:497
  2.2 118.2 %shard_map.55 = f32[32,1,128,128]{3,2,1,0:T(8,128)} custom-call(s32[8,128]{1,0:T(8,128)} %fusion.idx_ref, f32[24,1,128,128]{3,2,1,0:T(8,128)} %a_ref.1, f32[2,8,1,128,128]{4,3,2,1,0:T(8,128)} %b_ref.1), custom_call_target="tpu_custom_call" | custom-call | flops 10000000000 | bytes 10000000 | tf_op jit(solution)/shard_map/pallas_call | solution.py:504
  120.4 3.1 %copy.7 = f32[32,1,128,128]{3,2,1,0:T(8,128)} copy(f32[32,1,128,128]{3,2,1,0:T(8,128)} %shard_map.55) | data formatting | bytes 4194304
  (1 shorter events, 0.0 us)

commit v3 on v2

--- a/solution.py
+++ b/solution.py
@@ -328,40 +328,41 @@
     tab_copy.wait()
     low_copy.wait()
 
-    def multiply(zz, first, count):
+    def multiply(zz, first, count, outs):
         rows = count * PROW
+        unroll = UNROLL if len(outs) == 2 else UNROLL + UNROLL // 2
 
         def one(a):
             value = abuf[zz, first : first + count, a].reshape(rows, BLK)
             high = value.astype(jnp.bfloat16)
             low = (value - high.astype(jnp.float32)).astype(jnp.bfloat16)
-            both = jnp.concatenate([high, low], axis=0)
-            for o in (0, 1):
+            twice = [jnp.concatenate([part, part], axis=1) for part in (high, low)]
+            both = jnp.concatenate(twice, axis=0)
+            for o in outs:
                 b0 = low_s[2 * o, zz * LANE_A + a]
                 b1 = low_s[2 * o + 1, zz * LANE_A + a]
                 wide = jnp.concatenate([bhi[o, zz, b0], bhi[o, zz, b1]], axis=1)
                 fine = jnp.concatenate([blo[o, zz, b0], blo[o, zz, b1]], axis=1)
-                big = jnp.dot(both, wide, preferred_element_type=jnp.float32)
-                small = jnp.dot(high, fine, preferred_element_type=jnp.float32)
-                total = big[:rows] + (big[rows:] + small)
+                big = jnp.dot(both, jnp.concatenate([wide, fine], axis=0), preferred_element_type=jnp.float32)
+                total = big[:rows] + big[rows:]
                 for v in range(rows // SROW):
                     span = first * PROW // SROW + v
                     prods[span, o, 2 * a] = total[v * SROW : (v + 1) * SROW, :BLK]
                     prods[span, o, 2 * a + 1] = total[v * SROW : (v + 1) * SROW, BLK:]
 
         def some(i, carry):
-            for j in range(UNROLL):
-                one(i * UNROLL + j)
-            return carry
-
-        lax.fori_loop(0, ASLOT // UNROLL, some, 0)
+            for j in range(unroll):
+                one(i * unroll + j)
+            return carry
+
+        lax.fori_loop(0, ASLOT // unroll, some, 0)
 
     def gather(zz, o, spans, begin, end):
         base = o * (BLK // 2) + zz * BSLOT
 
         def some(i, carry):
-            for j in (0, 1):
-                s = i * 2 + j
+            for j in range(CSZ):
+                s = i * CSZ + j
                 at = [tab_s[s, base + b] for b in range(BSLOT)]
                 for v in spans:
                     terms = [prods[v, o, p] for p in at]
@@ -370,17 +371,24 @@
                     acc[v, o, s] += terms[0]
             return carry
 
-        lax.fori_loop(begin // 2, end // 2, some, 0)
-
-    def near(k, carry):
-        step = (k + 1) // 2
-        zz = (z + NZ + jnp.where(k % 2 == 1, step, -step)) % NZ
-        multiply(zz, 0, PARTS)
-        for o in (0, 1):
+        lax.fori_loop(begin // CSZ, end // CSZ, some, 0)
+
+    def near(o):
+        def one(k, carry):
+            step = (k + 1) // 2
+            zz = (z + NZ + jnp.where(k % 2 == 1, step, -step)) % NZ
+            multiply(zz, 0, PARTS, (o,))
             gather(zz, o, range(SPANS), 0, CSLOT)
-        return carry
-
-    lax.fori_loop(0, 5, near, 0)
+            return carry
+
+        lax.fori_loop(0, 5, one, 0)
+
+    near(1)
+    from_left(3, 2)
+    a_right(3, 2).start()
+    from_right(3, 2)
+    a_left(3, 2).start()
+    near(0)
 
     def c_piece(v, o, j):
         return acc.at[v, o, pl.ds(j * CSZ, CSZ)]
@@ -400,38 +408,52 @@
     def store_o(v, j):
         return pltpu.make_async_copy(c_piece(v, 0, j), out_piece(v, j, half), s_o.at[v, j])
 
-    far = ((z + 3) % NZ, (z + NZ - 3) % NZ)
+    def far(v, o):
+        def one(i, carry):
+            zz = (z + 3 + 2 * i) % NZ
+            multiply(zz, 2 * v, 2, (o,))
+            gather(zz, o, (v,), 0, CSLOT)
+            return carry
+
+        lax.fori_loop(0, 2, one, 0)
+
+    def finish(v, j):
+        landed(c_landing(v, j), r_c.at[v, j])
+
+        def add(s, carry):
+            acc[v, 0, s] += crecv[v, s]
+            return carry
+
+        lax.fori_loop(j * CSZ, (j + 1) * CSZ, add, 0)
+        send_m(v, j).start()
+        store_o(v, j).start()
+
     last = (z + 4) % NZ
     for v in range(SPANS):
-        if v == 0:
-            from_left(3, 2)
-            a_right(3, 2).start()
-            from_right(3, 2)
-            a_left(3, 2).start()
         from_left(3, 2 * v + 1)
         from_right(3, 2 * v + 1)
-        for zz in far:
-            multiply(zz, 2 * v, 2)
-            for o in (0, 1):
-                gather(zz, o, (v,), 0, CSLOT)
+        far(v, 1)
         from_left(4, 2 * v)
         from_right(4, 2 * v)
-        multiply(last, 2 * v, 2)
-        for j in range(CCH):
+        multiply(last, 2 * v, 2, (1,))
+
+        def give(j, carry):
             gather(last, 1, (v,), j * CSZ, (j + 1) * CSZ)
             send_c(v, j).start()
+            return carry
+
+        lax.fori_loop(0, CCH, give, 0)
+        if v:
+            finish(0, 2)
+            finish(0, 3)
+        far(v, 0)
+        multiply(last, 2 * v, 2, (0,))
         gather(last, 0, (v,), 0, CSLOT)
-    for v in range(SPANS):
-        for j in range(CCH):
-            landed(c_landing(v, j), r_c.at[v, j])
-
-            def add(s, carry):
-                acc[v, 0, s] += crecv[v, s]
-                return carry
-
-            lax.fori_loop(j * CSZ, (j + 1) * CSZ, add, 0)
-            send_m(v, j).start()
-            store_o(v, j).start()
+        if v == 0:
+            finish(0, 0)
+            finish(0, 1)
+    for j in range(CCH):
+        finish(1, j)
 
     for v in range(SPANS):
         for j in range(CCH):
@@ -485,7 +507,7 @@
     lax.fori_loop(0, PARTS, end_a, 0)
 
 
-UNROLL = 4
+UNROLL = 8
 
 
 def index_rows(a_index, b_index, c_index):

time: 124 us -> 113 us (0.911)
  Pallas kernels: 118 us -> 107 us
    pallas_call x1, Pallas kernels: 118 us -> 107 us  [local(): pl.pallas_call(kernel, out_shape=jax.ShapeDtypeStruct((CSLOT, 1, BLK, BLK...]
where the time goes in v3:
time: 113 us
  Pallas kernels  107 us (95%)
  local copies, waits for them, and re-layouts  3.98 us (4%)
  other arithmetic  1.36 us (1%)
    pallas_call x1, Pallas kernels, local(): pl.pallas_call(kernel, out_shape=jax.ShapeDtypeStruct((CSLOT, 1, BLK, BLK...  107 us
    unnamed x1, local copies, waits for them, and re-layouts  3.14 us

profile of v3, /device:TPU:1, one launch (start us, length us, event | category | flops | bytes accessed | tf_op | source)
XLA Modules:
  0.0 112.6 jit_solution(2615314446437188260)
XLA Ops:
  0.0 0.1 pad.23.clone
  0.1 0.7 pad.17
  0.8 0.1 reshape.3
  0.9 1.4 %fusion.idx_ref = s32[8,128]{1,0:T(8,128)} fusion(s32[2,32]{1,0:T(2,128)} %bitcast.4, s32[2,64]{1,0:T(2,128)S(1)} %reshape.3, s32[2,24]{1,0:T(2,128)} %bitcast.5, s32[8]{0:T(128)S(1)} %pad.23.clone), kind=kLoop, calls=%fused_computation.5 | loop fusion | flops 13312 | bytes 5088 | tf_op jit(solution)/shard_map/concatenate | solution.py:519
  2.2 107.3 %shard_map.55 = f32[32,1,128,128]{3,2,1,0:T(8,128)} custom-call(s32[8,128]{1,0:T(8,128)} %fusion.idx_ref, f32[24,1,128,128]{3,2,1,0:T(8,128)} %a_ref.1, f32[2,8,1,128,128]{4,3,2,1,0:T(8,128)} %b_ref.1), custom_call_target="tpu_custom_call" | custom-call | flops 10000000000 | bytes 10000000 | tf_op jit(solution)/shard_map/pallas_call | solution.py:526
  109.5 3.1 %copy.7 = f32[32,1,128,128]{3,2,1,0:T(8,128)} copy(f32[32,1,128,128]{3,2,1,0:T(8,128)} %shard_map.55) | data formatting | bytes 4194304
  (1 shorter events, 0.0 us)

commit v4 on v3

--- a/solution.py
+++ b/solution.py
@@ -303,26 +303,18 @@
     b_done(1, 1)
     b_done(1, 3)
     a_step(2, 0)
-    b_here(0, 2)
-    b_done(0, 2)
-    a_step(2, 1)
-    b_here(1, 2)
-    b_done(1, 2)
-    for j in (2, 3):
-        from_left(2, j)
-        from_right(2, j)
-    a_step(3, 0)
-    for j in (2, 3):
-        a_right(2, j).start()
-        a_left(2, j).start()
-
-    def take_b(i, carry):
-        o, zz = i // NY, (1 - q) * NY + i % NY
+
+    def take_b(o, i):
+        zz = (1 - q) * NY + (y + i) % NY
         landed(bbuf.at[o, zz], r_b.at[o, zz])
         split_b(o, zz)
-        return carry
-
-    lax.fori_loop(0, 2 * NY, take_b, 0)
+
+    def take_near(k, carry):
+        take_b(k // 3, (k % 3 + 3) % NY)
+        return carry
+
+    lax.fori_loop(0, 6, take_near, 0)
+    a_step(2, 1)
     for p in range(PARTS):
         local_a(p).wait()
     tab_copy.wait()
@@ -373,22 +365,43 @@
 
         lax.fori_loop(begin // CSZ, end // CSZ, some, 0)
 
-    def near(o):
-        def one(k, carry):
-            step = (k + 1) // 2
-            zz = (z + NZ + jnp.where(k % 2 == 1, step, -step)) % NZ
-            multiply(zz, 0, PARTS, (o,))
+    offset = (z + NY - y) % NY
+    one_first = jnp.where(offset == 2, 1, 0)
+    one_second = jnp.where((offset == 1) | (offset == 2), -1, 1)
+
+    def near(k, carry):
+        @pl.when(k == 1)
+        def _():
+            b_here(0, 2)
+            b_done(0, 2)
+            for j in (2, 3):
+                from_left(2, j)
+                from_right(2, j)
+
+        @pl.when(k == 2)
+        def _():
+            b_here(1, 2)
+            b_done(1, 2)
+            a_step(3, 0)
+            for j in (2, 3):
+                a_right(2, j).start()
+                a_left(2, j).start()
+            take_b(0, 2)
+            take_b(1, 2)
+
+        third = -one_first - one_second
+        by = jnp.where(k == 0, one_first, jnp.where(k == 1, one_second, jnp.where(k == 2, third, 14 - 4 * k)))
+        zz = (z + NZ + by) % NZ
+        multiply(zz, 0, PARTS, (0, 1))
+        for o in (0, 1):
             gather(zz, o, range(SPANS), 0, CSLOT)
-            return carry
-
-        lax.fori_loop(0, 5, one, 0)
-
-    near(1)
+        return carry
+
+    lax.fori_loop(0, 5, near, 0)
     from_left(3, 2)
     a_right(3, 2).start()
     from_right(3, 2)
     a_left(3, 2).start()
-    near(0)
 
     def c_piece(v, o, j):
         return acc.at[v, o, pl.ds(j * CSZ, CSZ)]

time: 113 us -> 105 us (0.929)
  Pallas kernels: 107 us -> 99.9 us
    pallas_call x1, Pallas kernels: 107 us -> 99.9 us  [local(): pl.pallas_call(kernel, out_shape=jax.ShapeDtypeStruct((CSLOT, 1, BLK, BLK...]
where the time goes in v4:
time: 105 us
  Pallas kernels  99.9 us (95%)
  local copies, waits for them, and re-layouts  3.98 us (4%)
  other arithmetic  1.36 us (1%)
    pallas_call x1, Pallas kernels, local(): pl.pallas_call(kernel, out_shape=jax.ShapeDtypeStruct((CSLOT, 1, BLK, BLK...  99.9 us
    unnamed x1, local copies, waits for them, and re-layouts  3.14 us

profile of v4, /device:TPU:1, one launch (start us, length us, event | category | flops | bytes accessed | tf_op | source)
XLA Modules:
  0.0 105.3 jit_solution(7965161582066383037)
XLA Ops:
  0.0 0.1 pad.23.clone
  0.1 0.7 pad.17
  0.8 0.1 reshape.3
  0.9 1.4 %fusion.idx_ref = s32[8,128]{1,0:T(8,128)} fusion(s32[2,32]{1,0:T(2,128)} %bitcast.4, s32[2,64]{1,0:T(2,128)S(1)} %reshape.3, s32[2,24]{1,0:T(2,128)} %bitcast.5, s32[8]{0:T(128)S(1)} %pad.23.clone), kind=kLoop, calls=%fused_computation.5 | loop fusion | flops 13312 | bytes 5088 | tf_op jit(solution)/shard_map/concatenate | solution.py:532
  2.2 99.9 %shard_map.55 = f32[32,1,128,128]{3,2,1,0:T(8,128)} custom-call(s32[8,128]{1,0:T(8,128)} %fusion.idx_ref, f32[24,1,128,128]{3,2,1,0:T(8,128)} %a_ref.1, f32[2,8,1,128,128]{4,3,2,1,0:T(8,128)} %b_ref.1), custom_call_target="tpu_custom_call" | custom-call | flops 10000000000 | bytes 10000000 | tf_op jit(solution)/shard_map/pallas_call | solution.py:539
  102.2 3.1 %copy.7 = f32[32,1,128,128]{3,2,1,0:T(8,128)} copy(f32[32,1,128,128]{3,2,1,0:T(8,128)} %shard_map.55) | data formatting | bytes 4194304
  (1 shorter events, 0.0 us)

commit v5 on v4

--- a/solution.py
+++ b/solution.py
@@ -442,29 +442,39 @@
         store_o(v, j).start()
 
     last = (z + 4) % NZ
-    for v in range(SPANS):
-        from_left(3, 2 * v + 1)
-        from_right(3, 2 * v + 1)
-        far(v, 1)
+
+    def give(v):
         from_left(4, 2 * v)
         from_right(4, 2 * v)
         multiply(last, 2 * v, 2, (1,))
 
-        def give(j, carry):
+        def one(j, carry):
             gather(last, 1, (v,), j * CSZ, (j + 1) * CSZ)
             send_c(v, j).start()
             return carry
 
-        lax.fori_loop(0, CCH, give, 0)
-        if v:
-            finish(0, 2)
-            finish(0, 3)
-        far(v, 0)
+        lax.fori_loop(0, CCH, one, 0)
+
+    def keep(v):
         multiply(last, 2 * v, 2, (0,))
         gather(last, 0, (v,), 0, CSLOT)
-        if v == 0:
-            finish(0, 0)
-            finish(0, 1)
+
+    from_left(3, 1)
+    from_right(3, 1)
+    far(0, 1)
+    give(0)
+    far(0, 0)
+    keep(0)
+    finish(0, 0)
+    from_left(3, 3)
+    from_right(3, 3)
+    far(1, 1)
+    finish(0, 1)
+    give(1)
+    finish(0, 2)
+    far(1, 0)
+    finish(0, 3)
+    keep(1)
     for j in range(CCH):
         finish(1, j)
 
@@ -524,22 +534,23 @@
 
 
 def index_rows(a_index, b_index, c_index):
-    def wide(part):
-        return jnp.pad(part, ((0, 0), (0, BLK - part.shape[1])), constant_values=-1)
-
-    b_rows = jnp.pad(b_index[..., 0], ((0, 0), (0, 0), (0, BLK // 4 - BSLOT)), constant_values=-1)
-    rows = [a_index[:, :, 0], b_rows.reshape(2, BLK // 2), c_index[:, :, 0], jnp.full((2, BLK), -1, jnp.int32)]
-    return jnp.concatenate([wide(part) for part in rows], axis=0)
+    def place(part, row, lane):
+        rows, lanes = part.shape
+        return lax.pad(part, jnp.int32(-1), ((row, 8 - row - rows, 0), (lane, BLK - lane - lanes, 0)))
+
+    ours = jnp.maximum(place(a_index[:, :, 0], 0, 0), place(b_index[:, 0, :, 0], 2, 0))
+    ours = jnp.maximum(ours, place(b_index[:, 1, :, 0], 2, BLK // 4))
+    return jnp.maximum(ours, place(c_index[:, :, 0], 4, 0))
 
 
 def local(a_blocks, a_index, b_blocks, b_index, c_index):
     dma = pltpu.SemaphoreType.DMA
     f32, bf16, i32 = jnp.float32, jnp.bfloat16, jnp.int32
-    anywhere = pl.BlockSpec(memory_space=pl.ANY)
+    anywhere, outside = pl.BlockSpec(memory_space=pl.ANY), pl.BlockSpec(memory_space=pltpu.HBM)
     return pl.pallas_call(
         kernel,
         out_shape=jax.ShapeDtypeStruct((CSLOT, 1, BLK, BLK), f32),
-        in_specs=[pl.BlockSpec(memory_space=pltpu.VMEM), anywhere, anywhere],
+        in_specs=[pl.BlockSpec(memory_space=pltpu.VMEM), outside, outside],
         out_specs=anywhere,
         scratch_shapes=[
             pltpu.VMEM((NZ, 8, BLK), i32),
@@ -562,7 +573,7 @@
             dma((SPANS, CCH)), dma((SPANS, CCH)), dma((SPANS, CCH)), dma((SPANS, CCH)), dma((SPANS, CCH)),
         ],
         compiler_params=pltpu.CompilerParams(
-            collective_id=0, has_side_effects=True, vmem_limit_bytes=56 * 1024 * 1024
+            collective_id=0, has_side_effects=True, vmem_limit_bytes=36 * 1024 * 1024
         ),
         cost_estimate=pl.CostEstimate(flops=10**10, bytes_accessed=10**7, transcendentals=0),
     )(index_rows(a_index, b_index, c_index), a_blocks, b_blocks)

time: 105 us -> 103 us (0.981)
  Pallas kernels: 99.9 us -> 97 us
    pallas_call x1, Pallas kernels: 99.9 us -> 97 us  [local(): pl.pallas_call(kernel, out_shape=jax.ShapeDtypeStruct((CSLOT, 1, BLK, BLK...]
    concatenate x1 -> x0, other arithmetic: 1.36 us -> none  [index_rows(): return jnp.concatenate([wide(part) for part in rows], axis=0)]
    unnamed x1 -> x5, local copies, waits for them, and re-layouts: 3.14 us -> 3.95 us
where the time goes in v5:
time: 103 us; the launch traced here: 102 us
  Pallas kernels  97 us (94%)
  local copies, waits for them, and re-layouts  4.65 us (5%)
    pallas_call x1, Pallas kernels, local(): pl.pallas_call(kernel, out_shape=jax.ShapeDtypeStruct((CSLOT, 1, BLK, BLK...  97 us
    unnamed x5, local copies, waits for them, and re-layouts  3.95 us

profile of v5, /device:TPU:1, one launch (start us, length us, event | category | flops | bytes accessed | tf_op | source)
XLA Modules:
  0.0 102.4 jit_solution(17941443846334337218)
XLA Ops:
  0.0 0.7 fusion
  0.7 0.8 pad_maximum_fusion.idx_ref
  1.5 0.0 copy-start
  1.5 1.4 %copy-done = f32[24,1,128,128]{3,2,1,0:T(8,128)S(1)} copy-done((f32[24,1,128,128]{3,2,1,0:T(8,128)S(1)}, f32[24,1,128,128]{3,2,1,0:T(8,128)}, u32[]{:S(2)}) %copy-start) | copy-done | bytes 1572888
  2.9 0.0 copy-start.1
  2.9 1.2 %copy-done.1 = f32[2,8,1,128,128]{4,3,2,1,0:T(8,128)S(1)} copy-done((f32[2,8,1,128,128]{4,3,2,1,0:T(8,128)S(1)}, f32[2,8,1,128,128]{4,3,2,1,0:T(8,128)}, u32[]{:S(2)}) %copy-start.1) | copy-done | bytes 1048600
  4.1 97.0 %shard_map.55 = f32[32,1,128,128]{3,2,1,0:T(8,128)S(1)} custom-call(s32[8,128]{1,0:T(8,128)S(1)} %pad_maximum_fusion.idx_ref, f32[24,1,128,128]{3,2,1,0:T(8,128)S(1)} %copy-done, f32[2,8,1,128,128]{4,3,2,1,0:T(8,128)S(1)} %copy-done.1), custom_call_target="tpu_custom_call" | custom-call | flops 10000000000 | bytes 10000000 | tf_op jit(solution)/shard_map/pallas_call | solution.py:550
  101.1 1.3 %copy.7 = f32[32,1,128,128]{3,2,1,0:T(8,128)} copy(f32[32,1,128,128]{3,2,1,0:T(8,128)S(1)} %shard_map.55) | data formatting | bytes 4194304
Async XLA Ops:
  1.5 1.4 %copy-start = (f32[24,1,128,128]{3,2,1,0:T(8,128)S(1)}, f32[24,1,128,128]{3,2,1,0:T(8,128)}, u32[]{:S(2)}) copy-start(f32[24,1,128,128]{3,2,1,0:T(8,128)} %a_ref.1) | copy-start | bytes 4718596
  2.9 1.2 %copy-start.1 = (f32[2,8,1,128,128]{4,3,2,1,0:T(8,128)S(1)}, f32[2,8,1,128,128]{4,3,2,1,0:T(8,128)}, u32[]{:S(2)}) copy-start(f32[2,8,1,128,128]{4,3,2,1,0:T(8,128)} %b_ref.1) | copy-start | bytes 3145732

commit v6 on v5

--- a/solution.py
+++ b/solution.py
@@ -23,7 +23,7 @@
     idx_a, idx_b, idx_c, tab_v, low_v, tab_s, low_s,
     abuf, bbuf, bhi, blo, prods, acc, crecv,
     s_ia, r_ia, s_ib, r_ib, s_ic, r_ic, s_tab,
-    s_al, s_ar, r_a, s_loc, s_bd, s_bn, s_bf, s_bx, r_b, s_c, r_c, s_o, s_m, r_m,
+    s_al, s_ar, r_a, s_loc, s_bd, s_bn, s_bf, s_bx, r_b, s_c, r_c, s_o, s_m, r_m, hello,
 ):
     r = lax.axis_index("row")
     c = lax.axis_index("col")
@@ -50,30 +50,12 @@
         pltpu.make_async_copy(ref, ref, sem).wait()
 
     barrier = pltpu.get_barrier_semaphore()
-
-    def greet(device):
+    near_by = [right, left, up, down, twin, partner, mate]
+    near_by += [(((y + i) % NY) * 2 + 1 - q, c, d) for i in (1, 3)]
+    near_by += [(y * 2 + 1 - q, z * 2 + 1 - h, 1 - d)]
+    for device in near_by:
         pl.semaphore_signal(barrier, inc=1, device_id=device, device_id_type=MESH)
-
-    def greet_z(i, carry):
-        greet((r, ((z + i) % NZ) * 2 + h, d))
-        return carry
-
-    lax.fori_loop(1, NZ, greet_z, 0)
-
-    def greet_b(i, carry):
-        yy = (y + i) % NY
-        greet((yy * 2 + h, z * 2 + 1 - h, 1 - d))
-
-        @pl.when(jnp.logical_not(own & (i == 0)))
-        def _():
-            greet((yy * 2 + h, c, d))
-
-        return carry
-
-    lax.fori_loop(0, NY, greet_b, 0)
-    for device in (partner, mate, twin, up, down):
-        greet(device)
-    pl.semaphore_wait(barrier, NZ - 1 + 2 * NY + 5 - own.astype(jnp.int32))
+    pl.semaphore_wait(barrier, len(near_by))
 
     def send_bd(i, s):
         yy = (y + i) % NY
@@ -136,6 +118,11 @@
         return carry
 
     lax.fori_loop(0, PARTS, start_a, 0)
+
+    for n in range(ROUNDS):
+        for device in near_by:
+            pl.semaphore_signal(hello.at[n], inc=1, device_id=device, device_id_type=MESH)
+        pl.semaphore_wait(hello.at[n], len(near_by))
 
     def send_ia(i):
         return remote(idx_ref, idx_a.at[z], s_ia.at[i], r_ia.at[z], (r, ((z + i) % NZ) * 2 + h, d))
@@ -531,6 +518,7 @@
 
 
 UNROLL = 8
+ROUNDS = 3
 
 
 def index_rows(a_index, b_index, c_index):
@@ -571,6 +559,7 @@
             dma((4, PARTS)), dma((4, PARTS)), dma((NZ, PARTS)), dma((PARTS,)),
             dma((NY, 2)), dma((2,)), dma((2,)), dma((2 * NY,)), dma((2, NZ)),
             dma((SPANS, CCH)), dma((SPANS, CCH)), dma((SPANS, CCH)), dma((SPANS, CCH)), dma((SPANS, CCH)),
+            pltpu.SemaphoreType.REGULAR((ROUNDS,)),
         ],
         compiler_params=pltpu.CompilerParams(
             collective_id=0, has_side_effects=True, vmem_limit_bytes=36 * 1024 * 1024

time: 103 us -> 102 us (level)
  no operation moved by 1% of the time
where the time goes in v6:
time: 102 us
  Pallas kernels  96.7 us (95%)
  local copies, waits for them, and re-layouts  4.65 us (5%)
    pallas_call x1, Pallas kernels, local(): pl.pallas_call(kernel, out_shape=jax.ShapeDtypeStruct((CSLOT, 1, BLK, BLK...  96.7 us
    unnamed x5, local copies, waits for them, and re-layouts  3.95 us

profile of v6, /device:TPU:1, one launch (start us, length us, event | category | flops | bytes accessed | tf_op | source)
XLA Modules:
  0.0 102.1 jit_solution(3976495821253981323)
XLA Ops:
  0.0 0.7 fusion
  0.7 0.8 pad_maximum_fusion.idx_ref
  1.5 0.0 copy-start
  1.5 1.4 %copy-done = f32[24,1,128,128]{3,2,1,0:T(8,128)S(1)} copy-done((f32[24,1,128,128]{3,2,1,0:T(8,128)S(1)}, f32[24,1,128,128]{3,2,1,0:T(8,128)}, u32[]{:S(2)}) %copy-start) | copy-done | bytes 1572888
  2.9 0.0 copy-start.1
  2.9 1.2 %copy-done.1 = f32[2,8,1,128,128]{4,3,2,1,0:T(8,128)S(1)} copy-done((f32[2,8,1,128,128]{4,3,2,1,0:T(8,128)S(1)}, f32[2,8,1,128,128]{4,3,2,1,0:T(8,128)}, u32[]{:S(2)}) %copy-start.1) | copy-done | bytes 1048600
  4.1 96.7 %shard_map.55 = f32[32,1,128,128]{3,2,1,0:T(8,128)S(1)} custom-call(s32[8,128]{1,0:T(8,128)S(1)} %pad_maximum_fusion.idx_ref, f32[24,1,128,128]{3,2,1,0:T(8,128)S(1)} %copy-done, f32[2,8,1,128,128]{4,3,2,1,0:T(8,128)S(1)} %copy-done.1), custom_call_target="tpu_custom_call" | custom-call | flops 10000000000 | bytes 10000000 | tf_op jit(solution)/shard_map/pallas_call | solution.py:538
  100.8 1.3 %copy.7 = f32[32,1,128,128]{3,2,1,0:T(8,128)} copy(f32[32,1,128,128]{3,2,1,0:T(8,128)S(1)} %shard_map.55) | data formatting | bytes 4194304
Async XLA Ops:
  1.5 1.4 %copy-start = (f32[24,1,128,128]{3,2,1,0:T(8,128)S(1)}, f32[24,1,128,128]{3,2,1,0:T(8,128)}, u32[]{:S(2)}) copy-start(f32[24,1,128,128]{3,2,1,0:T(8,128)} %a_ref.1) | copy-start | bytes 4718596
  2.9 1.2 %copy-start.1 = (f32[2,8,1,128,128]{4,3,2,1,0:T(8,128)S(1)}, f32[2,8,1,128,128]{4,3,2,1,0:T(8,128)}, u32[]{:S(2)}) copy-start(f32[2,8,1,128,128]{4,3,2,1,0:T(8,128)} %b_ref.1) | copy-start | bytes 3145732

commit v7 on v6

--- a/solution.py
+++ b/solution.py
@@ -13,7 +13,9 @@
 ROWS = BLK // 2
 PARTS, PROW = 4, ROWS // 4
 SPANS, SROW = 2, ROWS // 2
-CCH, CSZ = 4, CSLOT // 4
+CCH, CSZ = 8, CSLOT // 8
+UNROLL = 8
+ROUNDS = 3
 LANE_A = 32
 ZERO = 2 * ASLOT
 
@@ -336,12 +338,12 @@
 
         lax.fori_loop(0, ASLOT // unroll, some, 0)
 
-    def gather(zz, o, spans, begin, end):
+    def gather(zz, o, spans, begin, end, unroll=UNROLL):
         base = o * (BLK // 2) + zz * BSLOT
 
         def some(i, carry):
-            for j in range(CSZ):
-                s = i * CSZ + j
+            for j in range(unroll):
+                s = i * unroll + j
                 at = [tab_s[s, base + b] for b in range(BSLOT)]
                 for v in spans:
                     terms = [prods[v, o, p] for p in at]
@@ -350,7 +352,7 @@
                     acc[v, o, s] += terms[0]
             return carry
 
-        lax.fori_loop(begin // CSZ, end // CSZ, some, 0)
+        lax.fori_loop(begin // unroll, end // unroll, some, 0)
 
     offset = (z + NY - y) % NY
     one_first = jnp.where(offset == 2, 1, 0)
@@ -436,7 +438,7 @@
         multiply(last, 2 * v, 2, (1,))
 
         def one(j, carry):
-            gather(last, 1, (v,), j * CSZ, (j + 1) * CSZ)
+            gather(last, 1, (v,), j * CSZ, (j + 1) * CSZ, CSZ)
             send_c(v, j).start()
             return carry
 
@@ -453,14 +455,18 @@
     far(0, 0)
     keep(0)
     finish(0, 0)
+    finish(0, 1)
     from_left(3, 3)
     from_right(3, 3)
     far(1, 1)
-    finish(0, 1)
+    finish(0, 2)
+    finish(0, 3)
     give(1)
-    finish(0, 2)
+    finish(0, 4)
+    finish(0, 5)
     far(1, 0)
-    finish(0, 3)
+    finish(0, 6)
+    finish(0, 7)
     keep(1)
     for j in range(CCH):
         finish(1, j)
@@ -515,10 +521,6 @@
         return carry
 
     lax.fori_loop(0, PARTS, end_a, 0)
-
-
-UNROLL = 8
-ROUNDS = 3
 
 
 def index_rows(a_index, b_index, c_index):

time: 102 us -> 102 us (level)
  no operation moved by 1% of the time
where the time goes in v7:
time: 102 us; the launch traced here: 101 us
  Pallas kernels  95.7 us (94%)
  local copies, waits for them, and re-layouts  4.65 us (5%)
    pallas_call x1, Pallas kernels, local(): pl.pallas_call(kernel, out_shape=jax.ShapeDtypeStruct((CSLOT, 1, BLK, BLK...  95.7 us
    unnamed x5, local copies, waits for them, and re-layouts  3.95 us

profile of v7, /device:TPU:1, one launch (start us, length us, event | category | flops | bytes accessed | tf_op | source)
XLA Modules:
  0.0 101.1 jit_solution(15239013819635168070)
XLA Ops:
  0.0 0.7 fusion
  0.7 0.8 pad_maximum_fusion.idx_ref
  1.5 0.0 copy-start
  1.5 1.4 %copy-done = f32[24,1,128,128]{3,2,1,0:T(8,128)S(1)} copy-done((f32[24,1,128,128]{3,2,1,0:T(8,128)S(1)}, f32[24,1,128,128]{3,2,1,0:T(8,128)}, u32[]{:S(2)}) %copy-start) | copy-done | bytes 1572888
  2.9 0.0 copy-start.1
  2.9 1.2 %copy-done.1 = f32[2,8,1,128,128]{4,3,2,1,0:T(8,128)S(1)} copy-done((f32[2,8,1,128,128]{4,3,2,1,0:T(8,128)S(1)}, f32[2,8,1,128,128]{4,3,2,1,0:T(8,128)}, u32[]{:S(2)}) %copy-start.1) | copy-done | bytes 1048600
  4.1 95.7 %shard_map.55 = f32[32,1,128,128]{3,2,1,0:T(8,128)S(1)} custom-call(s32[8,128]{1,0:T(8,128)S(1)} %pad_maximum_fusion.idx_ref, f32[24,1,128,128]{3,2,1,0:T(8,128)S(1)} %copy-done, f32[2,8,1,128,128]{4,3,2,1,0:T(8,128)S(1)} %copy-done.1), custom_call_target="tpu_custom_call" | custom-call | flops 10000000000 | bytes 10000000 | tf_op jit(solution)/shard_map/pallas_call | solution.py:540
  99.8 1.3 %copy.7 = f32[32,1,128,128]{3,2,1,0:T(8,128)} copy(f32[32,1,128,128]{3,2,1,0:T(8,128)S(1)} %shard_map.55) | data formatting | bytes 4194304
Async XLA Ops:
  1.5 1.4 %copy-start = (f32[24,1,128,128]{3,2,1,0:T(8,128)S(1)}, f32[24,1,128,128]{3,2,1,0:T(8,128)}, u32[]{:S(2)}) copy-start(f32[24,1,128,128]{3,2,1,0:T(8,128)} %a_ref.1) | copy-start | bytes 4718596
  2.9 1.2 %copy-start.1 = (f32[2,8,1,128,128]{4,3,2,1,0:T(8,128)S(1)}, f32[2,8,1,128,128]{4,3,2,1,0:T(8,128)}, u32[]{:S(2)}) copy-start(f32[2,8,1,128,128]{4,3,2,1,0:T(8,128)} %b_ref.1) | copy-start | bytes 3145732
